TPU v7x, 128 devices: a whole 4x4x4 slice. The times are simulated.
128 devices in a mesh: row: 8 (over y_hi, z), col: 16 (over x, y_lo, core).
Axes of the slice: x: 4, y: 4 (y_hi: 2, y_lo: 2; y = y_hi * 2 + y_lo), z: 4, core: 2. Of those that a mesh axis runs over, the one named last changes fastest.
Arguments:
- homolog_features: bfloat16 [64, 704, 256], P('col', 'row'), may hold values from -6 to 6
- pair_state: bfloat16 [704, 704, 128], P('row', 'col'), may hold values from -6 to 6
- first_factor_matrix: bfloat16 [256, 32], replicated, may hold values from -0.375 to 0.375
- second_factor_matrix: bfloat16 [256, 32], replicated, may hold values from -0.375 to 0.375
- outer_pair_weight: bfloat16 [1024, 128], replicated, may hold values from -1.5 to 1.5
- triangle_left_weight: bfloat16 [128, 256], replicated, may hold values from -0.5 to 0.5
- triangle_right_weight: bfloat16 [128, 256], replicated, may hold values from -0.5 to 0.5
- triangle_gate_weight: bfloat16 [128, 128], replicated, may hold values from -0.5 to 0.5
- triangle_output_weight: bfloat16 [128, 128], replicated, may hold values from -0.5 to 0.5
Outputs:
- pair_out: bfloat16 [704, 704, 128], P('row', 'col')
All inputs are finite; a program needn't handle non-finite values.
Results may differ from a plain program's by a relative error of at most 0.0069.
Values may be sent and summed in bfloat16 or wider, within the bound.
A program may use at most 128 MiB of HBM per device.

v0:
```python
import math

import jax
import jax.numpy as jnp
from jax import lax
from jax.sharding import PartitionSpec as P


def spread(shard, axis, root):
    mine = lax.axis_index(axis) == root
    return lax.psum(jnp.where(mine, shard, jnp.zeros_like(shard)), axis)


def apply_layer_norm(values, reduce_axis):
    average = jnp.mean(values, axis=reduce_axis, keepdims=True)
    centered = values - average
    variance = jnp.mean(centered * centered, axis=reduce_axis, keepdims=True)
    return centered * lax.rsqrt(variance + 1e-05)


def per_device(
    homolog_features,
    pair_state,
    first_factor_matrix,
    second_factor_matrix,
    outer_pair_weight,
    triangle_left_weight,
    triangle_right_weight,
    triangle_gate_weight,
    triangle_output_weight,
):
    row_count = pair_state.shape[0]
    col_count = pair_state.shape[1]
    hidden = triangle_output_weight.shape[0]
    per_row = lax.axis_size("col") // lax.axis_size("row")
    col_index = lax.axis_index("col")
    root_row = col_index // per_row
    row_offset = col_index % per_row * col_count
    alignment_norm = apply_layer_norm(homolog_features.astype(jnp.float32), -1).astype(jnp.bfloat16)
    left_alignment = jnp.einsum(
        "mgu,ur->mgr", alignment_norm, first_factor_matrix, preferred_element_type=jnp.float32
    ).astype(jnp.bfloat16)
    right_alignment = jnp.einsum(
        "mgu,ur->mgr", alignment_norm, second_factor_matrix, preferred_element_type=jnp.float32
    ).astype(jnp.bfloat16)
    sequence_left = lax.all_gather(left_alignment, "col", axis=0, tiled=True)
    sequence_gathered = lax.all_gather(right_alignment, "col", axis=0, tiled=True)
    own_columns = lax.dynamic_slice_in_dim(sequence_gathered, row_offset, col_count, 1)
    seq_right = spread(own_columns, "row", root_row)
    seq_total = sequence_left.shape[0]
    block_slice = math.gcd(row_count, 8)

    def outer_block(slice_index):
        left_block_slice = lax.dynamic_slice_in_dim(
            sequence_left, slice_index * block_slice, block_slice, 1
        )
        outer_sum = jnp.einsum(
            "rhp,rmw->hmpw", left_block_slice, seq_right, preferred_element_type=jnp.float32
        ) * (1.0 / seq_total)
        flat = outer_sum.astype(jnp.bfloat16).reshape(block_slice, col_count, -1)
        return jnp.einsum(
            "ijf,fz->ijz", flat, outer_pair_weight, preferred_element_type=jnp.float32
        )

    update = lax.map(outer_block, jnp.arange(row_count // block_slice, dtype=jnp.int32)).reshape(
        row_count, col_count, -1
    )
    pair_mid = pair_state.astype(jnp.float32) + update
    pair_norm = apply_layer_norm(pair_mid, -1).astype(jnp.bfloat16)
    left_proj = jnp.einsum(
        "ijd,dc->cij", pair_norm, triangle_left_weight, preferred_element_type=jnp.float32
    )
    right_proj = jnp.einsum(
        "ijd,dc->cij", pair_norm, triangle_right_weight, preferred_element_type=jnp.float32
    )
    left_edge = (jax.nn.sigmoid(left_proj[:hidden]) * left_proj[hidden:]).astype(jnp.bfloat16)
    right_edge = (jax.nn.sigmoid(right_proj[:hidden]) * right_proj[hidden:]).astype(jnp.bfloat16)
    edge_gathered = lax.all_gather(right_edge, "col", axis=2, tiled=True)
    own_rows = lax.dynamic_slice_in_dim(edge_gathered, row_offset, col_count, 1)
    key_rows = spread(own_rows, "row", root_row)
    combined = jnp.einsum(
        "cik,cjk->cij",
        lax.all_gather(left_edge, "col", axis=2, tiled=True),
        key_rows,
        preferred_element_type=jnp.float32,
    )
    combined_norm = apply_layer_norm(combined, 0).astype(jnp.bfloat16)
    gating = jax.nn.sigmoid(
        jnp.einsum(
            "ijd,dz->ijz", pair_norm, triangle_gate_weight, preferred_element_type=jnp.float32
        )
    )
    branch = jnp.einsum(
        "cij,cz->ijz", combined_norm, triangle_output_weight, preferred_element_type=jnp.float32
    )
    return (pair_mid + gating * branch).astype(jnp.bfloat16)


def solution(mesh):
    return jax.shard_map(
        per_device,
        mesh=mesh,
        in_specs=(P("col", "row", None), P("row", "col", None), P(), P(), P(), P(), P(), P(), P()),
        out_specs=P("row", "col", None),
        check_vma=False,
    )
```

profile of v0, /device:TPU:1, one launch (start us, length us, event | category | flops | bytes accessed | tf_op | source)
XLA Modules:
  0.0 718.1 jit_solution(14508220906993592618)
XLA Ops:
  10.1 22.5 %all_gather.13 = bf16[64,88,32]{1,2,0:T(8,128)(2,1)S(1)} all-gather(bf16[4,88,32]{1,2,0:T(8,128)(2,1)S(1)} %convolution_convert_fusion), channel_id=1, replica_groups=mesh['row'=8,'col'=16] {'col'}, dimensions={0}, use_global_device_ids=true | all-gather | bytes 382976 | tf_op jit(solution)/shard_map/all_gather | solution.py:47
  33.9 17.7 %all_gather.12 = bf16[64,88,32]{1,2,0:T(8,128)(2,1)S(1)} all-gather(bf16[4,88,32]{1,2,0:T(8,128)(2,1)S(1)} %convolution_convert_fusion.1), channel_id=1, replica_groups=mesh['row'=8,'col'=16] {'col'}, dimensions={0}, use_global_device_ids=true | all-gather | bytes 382976 | tf_op jit(solution)/shard_map/all_gather | solution.py:46
  53.8 59.8 %all-reduce.3.cloned.1.call-done = bf16[64,44,32]{1,2,0:T(8,128)(2,1)} async-done(((bf16[64,44,32]{1,2,0:T(8,128)(2,1)}), bf16[64,44,32]{1,2,0:T(8,128)(2,1)}) %all-reduce.3.cloned.1.call-update) | async-done | bytes 180240 | tf_op jit(solution)/shard_map/psum | solution.py:11
  115.3 182.2 %while.10 = (s32[]{:T(128)}, f32[11,8,44,128]{3,1,0,2:T(8,128)}, s32[11]{0:T(128)S(1)}, bf16[64,88,32]{0,2,1:T(8,128)(2,1)}, bf16[64,44,32]{0,1,2:T(8,128)(2,1)S...) while((s32[]{:T(128)}, f32[11,8,44,128]{3,1,0,2:T(8,128)}, ...), condition=%wide.region_4.5_spmd, body=%wide.region_3.4_spmd.sunk | while | flops 139132928 | bytes 5014179 | solution.py:65
  119.5 6.4 copy.44
  126.0 3.7 reshape.55
  136.1 6.4 copy.44
  152.7 6.4 copy.44
  169.3 6.4 copy.44
  185.8 6.4 copy.44
  202.4 6.4 copy.44
  218.9 6.4 copy.44
  235.5 6.4 copy.44
  252.0 6.4 copy.44
  268.6 6.4 copy.44
  285.1 6.4 copy.44
  308.0 88.3 %all-gather.5.cloned.1.call-done = bf16[128,88,704]{0,1,2:T(8,128)(2,1)} async-done(((bf16[128,88,44]{0,1,2:T(8,128)(2,1)}), bf16[128,88,704]{0,1,2:T(8,128)(2,1)}) %all-gather.5.cloned.1.call-update) | async-done | bytes 15859728 | tf_op jit(solution)/shard_map/all_gather | solution.py:78
  396.3 12.1 %constant_dynamic-slice_fusion = bf16[128,44,704]{0,1,2:T(8,128)(2,1)} fusion(bf16[128,88,704]{0,1,2:T(8,128)(2,1)} %all-gather.5.cloned.1.call-done, s32[]{:T(128)S(6)} %select_n.37), kind=kLoop, calls=%fused_computation.54 | loop fusion | bytes 15859716 | tf_op jit(solution)/shard_map/dynamic_slice | solution.py:79
  408.4 14.0 %copy.34 = bf16[128,44,704]{2,1,0:T(8,128)(2,1)} copy(bf16[128,44,704]{0,1,2:T(8,128)(2,1)} %constant_dynamic-slice_fusion) | data formatting | bytes 15859712
  422.4 8.0 %broadcast_select_fusion = bf16[128,44,704]{2,1,0:T(8,128)(2,1)} fusion(bf16[128,44,704]{2,1,0:T(8,128)(2,1)} %copy.34, pred[]{:T(512)S(6)} %eq.6), kind=kLoop, calls=%fused_computation.9 | loop fusion | flops 3964928 | bytes 15859713 | tf_op jit(solution)/shard_map/jit(_where)/select_n | solution.py:11
  433.1 53.1 %all-gather.3.cloned.1.call-done = bf16[128,88,704]{0,1,2:T(8,128)(2,1)} async-done(((bf16[128,88,44]{0,1,2:T(8,128)(2,1)}), bf16[128,88,704]{0,1,2:T(8,128)(2,1)}) %all-gather.3.cloned.1.call-update) | async-done | bytes 15859728 | tf_op jit(solution)/shard_map/all_gather | solution.py:83
  486.3 27.3 %copy.29 = bf16[128,88,704]{1,2,0:T(8,128)(2,1)} copy(bf16[128,88,704]{0,1,2:T(8,128)(2,1)} %all-gather.3.cloned.1.call-done) | data formatting | bytes 31719424 | tf_op jit(solution)/shard_map/all_gather | solution.py:83
  513.6 181.5 %all-reduce.5.cloned.1.call-done = bf16[128,44,704]{2,1,0:T(8,128)(2,1)} async-done(((bf16[128,44,704]{2,1,0:T(8,128)(2,1)}), bf16[128,44,704]{2,1,0:T(8,128)(2,1)}) %all-reduce.5.cloned.1.call-update) | async-done | bytes 7929872 | tf_op jit(solution)/shard_map/psum | solution.py:11
  695.1 11.9 %fusion.30 = (f32[88,44]{0,1:T(8,128)S(1)}, f32[128,88,44]{1,2,0:T(8,128)S(1)}) fusion(bf16[128,88,704]{1,2,0:T(8,128)(2,1)} %copy.29, bf16[128,44,704]{2,1,0:T(8,128)(2,1)} %all-reduce.5.cloned.1.call-done), kind=kOutput, calls=%fused_computation.55 | convolution fusion | flops 698319104 | bytes 25787520 | tf_op jit(solution)/shard_map/cik,cjk->cij/dot_general | solution.py:81
  (99 shorter events, 126.7 us)
Async XLA Ops:
  6.5 296.9 %copy-start = (bf16[128,256]{1,0:T(8,128)(2,1)S(1)}, bf16[128,256]{1,0:T(8,128)(2,1)}, u32[]{:S(2)}) copy-start(bf16[128,256]{1,0:T(8,128)(2,1)} %param.17) | copy-start | bytes 196612
  6.5 27.1 %copy-start.6 = (bf16[4,88,256]{2,1,0:T(8,128)(2,1)S(1)}, bf16[4,88,256]{2,1,0:T(8,128)(2,1)}, u32[]{:S(2)}) copy-start(bf16[4,88,256]{2,1,0:T(8,128)(2,1)} %param.11) | copy-start | bytes 540676
  6.5 27.1 %copy-start.10 = (bf16[256,32]{0,1:T(8,128)(2,1)S(1)}, bf16[256,32]{0,1:T(8,128)(2,1)}, u32[]{:S(2)}) copy-start(bf16[256,32]{0,1:T(8,128)(2,1)} %param.13) | copy-start | bytes 49156
  6.5 107.1 %all-reduce.3.cloned.1.call-start = ((), (), s32[]{:S(2)}) async-start(), calls=%async_computation | async-start | bytes 1048576 | tf_op jit(solution)/shard_map/psum | solution.py:11
  33.6 362.7 %all-gather.5.cloned.1.call-start = ((), (), s32[]{:S(2)}) async-start(), calls=%async_computation.2 | async-start | bytes 16850944 | tf_op jit(solution)/shard_map/all_gather | solution.py:78
  297.5 2.8 copy-start.2
  297.6 2.8 copy-start.3
  304.1 1.6 copy-start.7
  305.6 180.7 %all-gather.3.cloned.1.call-start = ((), (), s32[]{:S(2)}) async-start(), calls=%async_computation.1 | async-start | bytes 16850944 | tf_op jit(solution)/shard_map/all_gather | solution.py:83
  307.8 387.3 %all-reduce.5.cloned.1.call-start = ((), (), s32[]{:S(2)}) async-start(), calls=%async_computation.3 | async-start | bytes 18874368 | tf_op jit(solution)/shard_map/psum | solution.py:11
  430.4 0.8 copy-start.8
  707.5 1.2 copy-start.4
  707.5 1.9 copy-start.5
  707.5 1.8 copy-start.9
  709.4 2.1 copy-start.1
Sparse Core Ops, SparseCore 0:
  33.7 79.8 all-reduce.2
  305.7 90.5 all-gather.4
  398.1 88.0 all-gather.2
  488.8 206.2 all-reduce.4
where the time goes:
time: 721 us; the launch traced here: 718 us
  waiting for transfers between devices  383 us (53%)
  local copies, waits for them, and re-layouts  178 us (25%)
  matrix products  75.4 us (10%)
  blocking collectives  40.2 us (6%)
  other arithmetic  20.9 us (3%)
  between operations  13.3 us (2%)
  loops' own time  7.21 us (1%)
    psum x2, waiting for transfers between devices, spread(): return lax.psum(jnp.where(mine, shard, jnp.zeros_like(shard)), axis)  241 us
    all_gather x1, waiting for transfers between devices, per_device(): edge_gathered = lax.all_gather(right_edge, 'col', axis=2, tiled=True)  88.3 us
    convert_element_type x11, local copies, waits for them, and re-layouts, outer_block(): flat = outer_sum.astype(jnp.bfloat16).reshape(block_slice, col_count, -1)  70.8 us
    all_gather x1, waiting for transfers between devices, per_device(): lax.all_gather(left_edge, 'col', axis=2, tiled=True)  53.1 us
    reshape x11, local copies, waits for them, and re-layouts, outer_block(): flat = outer_sum.astype(jnp.bfloat16).reshape(block_slice, col_count, -1)  40.9 us
    dot_general x11, matrix products, outer_block(): jnp.einsum('rhp,rmw->hmpw', left_block_slice, seq_right, preferred_elemen...  32.1 us
    all_gather x1, local copies, waits for them, and re-layouts, per_device(): lax.all_gather(left_edge, 'col', axis=2, tiled=True)  27.3 us
    dot_general x11, matrix products, outer_block(): jnp.einsum('ijf,fz->ijz', flat, outer_pair_weight, preferred_element_type...  24.5 us
  transfers between devices with their start and end apart: 4, of which 4 were waited for; matrix products, arithmetic and copies ran while one was open for 9% of the time, Pallas kernels for 0%

commit v1 on v0

v1 whole, which is shorter than its diff:
```python
import jax
import jax.numpy as jnp
from jax import lax
from jax.experimental import pallas as pl
from jax.experimental.pallas import tpu as pltpu
from jax.sharding import PartitionSpec as P

ROWS, COLS = 8, 16
N = ROWS * COLS
RI, CJ = 88, 44
MESH = pl.DeviceIdType.MESH
VM = pl.BlockSpec(memory_space=pltpu.VMEM)
F32, BF = jnp.float32, jnp.bfloat16
NT = (((1,), (1,)), ((), ()))
TN = (((0,), (0,)), ((), ()))


def dev(flat):
    return (flat // COLS, flat % COLS)


def mixed(me, step):
    u = (step * 37) % 128
    a, b, c, dk = u % 4, (u // 4) % 4, (u // 16) % 4, u // 64
    row, col = me // COLS, me % COLS
    x, y, z, k = col // 4, (row // 4) * 2 + (col // 2) % 2, row % 4, col % 2
    x, y, z, k = (x + a) % 4, (y + a + b) % 4, (z + a + c) % 4, (k + dk) % 2
    return ((y // 2) * 4 + z) * COLS + x * 4 + (y % 2) * 2 + k


def sigmoid(v):
    return 0.5 * jnp.tanh(0.5 * v) + 0.5


def msa_kernel(hf, f1p, f2p, l_out, r_out, a_ref, p_ref, ls, rs, ssl, ssr, rsl, rsr):
    row, col = lax.axis_index("row"), lax.axis_index("col")
    sem = pltpu.get_barrier_semaphore()

    def greet(s, _):
        t = (col + s) % COLS
        pl.semaphore_signal(sem, inc=1, device_id=(row, t), device_id_type=MESH)
        return 0

    lax.fori_loop(1, COLS, greet, 0)

    def greet_source(s, _):
        own = jnp.logical_and(row == col // 2, s == col)

        @pl.when(jnp.logical_not(own))
        def _():
            pl.semaphore_signal(sem, inc=1, device_id=(col // 2, s), device_id_type=MESH)

        return 0

    lax.fori_loop(0, COLS, greet_source, 0)

    v = hf[...].astype(F32)
    centered = v - jnp.mean(v, axis=-1, keepdims=True)
    mn = centered * lax.rsqrt(jnp.mean(centered * centered, axis=-1, keepdims=True) + 1e-05)
    for s in range(4):
        for g in range(22):
            qt, q = g // 4, g % 4
            a_ref[qt * 16 + s * 4 : qt * 16 + s * 4 + 4, q * 256 : q * 256 + 256] = mn[s, g * 4 : g * 4 + 4]
    a_ref[80:96, 512:1024] = jnp.zeros((16, 512), F32)
    lm = jnp.dot(a_ref[...].astype(BF), f1p[...], preferred_element_type=F32)
    for qt in range(6):
        ls[:, qt * 128 : qt * 128 + 128] = lm[qt * 16 : qt * 16 + 16].astype(BF)
    pr = jnp.dot(
        jnp.concatenate([mn[s] for s in range(4)], axis=1).astype(BF), f2p[...], preferred_element_type=F32
    )
    p_ref[...] = jnp.zeros(p_ref.shape, F32)
    p_ref[0:44] = pr[0:44]
    p_ref[64:108] = pr[44:88]
    tr = p_ref[...].T
    for h in range(2):
        rs[h] = jnp.concatenate(
            [tr[eg * 16 : eg * 16 + 16, h * 64 : h * 64 + 48] for eg in range(8)], axis=1
        ).astype(BF)

    own_source = (row == col // 2).astype(jnp.int32)
    pl.semaphore_wait(sem, (COLS - 1) + 2 * ROWS - own_source)

    own = pl.ds(pl.multiple_of(col * 16, 16), 16)
    keep = pltpu.make_async_copy(ls, l_out.at[own], rsl)
    keep.start()

    def left(s):
        return pltpu.make_async_remote_copy(
            src_ref=ls, dst_ref=l_out.at[own], send_sem=ssl.at[s], recv_sem=rsl,
            device_id=(row, (col + s) % COLS), device_id_type=MESH,
        )

    def right(s):
        h, t = s % 2, (row + s // 2) % ROWS
        return pltpu.make_async_remote_copy(
            src_ref=rs.at[h], dst_ref=r_out.at[own], send_sem=ssr.at[s], recv_sem=rsr,
            device_id=(t, 2 * row + h), device_id_type=MESH,
        )

    def mine(s):
        return jnp.logical_and(s // 2 == 0, col == 2 * row + s % 2)

    def send_right(s, _):
        @pl.when(jnp.logical_not(mine(s)))
        def _():
            right(s).start()

        @pl.when(mine(s))
        def _():
            pltpu.make_async_copy(rs.at[s % 2], r_out.at[own], rsr).start()

        return 0

    def send_left(s, _):
        left(s).start()
        return 0

    lax.fori_loop(1, COLS, send_left, 0)
    lax.fori_loop(0, 2 * ROWS, send_right, 0)

    def sent_left(s, _):
        left(s).wait_send()
        return 0

    def sent_right(s, _):
        @pl.when(jnp.logical_not(mine(s)))
        def _():
            right(s).wait_send()

        return 0

    pltpu.make_async_copy(l_out, l_out, rsl).wait()
    pltpu.make_async_copy(r_out, r_out, rsr).wait()
    lax.fori_loop(1, COLS, sent_left, 0)
    lax.fori_loop(0, 2 * ROWS, sent_right, 0)


def iota(shape, dim):
    return lax.broadcasted_iota(jnp.int32, shape, dim)


def pair_kernel(lmsg, rmsg, ps, wt, wedge, wgate, send, mid, gate, rmt, bd, lhs, osc, pn, el, er):
    rmt[...] = rmsg[...].T
    bd[...] = jnp.zeros(bd.shape, BF)

    def place(e, _):
        for q in range(4):
            bd[pl.ds(pl.multiple_of(e * 128 + q * 32, 32), 32), q * 128 : q * 128 + 128] = wt[
                pl.ds(pl.multiple_of(e * 32, 32), 32), :
            ]
        return 0

    lax.fori_loop(0, 32, place, 0)

    def outer(uw, _):
        u, w = uw // 4, uw % 4
        a, b = iota((256, 256), 0), iota((256, 256), 1)
        pick = (a // 4 == b // 4) & (a % 4 == w) & (b % 4 == u)
        sel = jnp.dot(rmt[...], pick.astype(F32).astype(BF), preferred_element_type=F32).astype(BF)
        x = jnp.dot(sel, lmsg[...], preferred_element_type=F32) * (1.0 / 64)
        for eg in range(8):
            for qt in range(6):
                lhs[
                    pl.ds(pl.multiple_of(u * 288 + qt * 48, 16), 48),
                    pl.ds(pl.multiple_of(w * 1024 + eg * 128, 128), 128),
                ] = x[eg * 48 : eg * 48 + 48, qt * 128 : qt * 128 + 128].astype(BF)
        return 0

    lax.fori_loop(0, 16, outer, 0)

    def project(u, _):
        rows = pl.ds(pl.multiple_of(u * 288, 16), 288)
        osc[rows, :] = jnp.dot(lhs[rows, :], bd[...], preferred_element_type=F32)
        return 0

    lax.fori_loop(0, 4, project, 0)

    def normalize(ia, _):
        for ib in range(11):
            upd = osc[
                pl.ds(pl.multiple_of((ia % 4) * 288 + (ib // 2) * 48, 8), 48),
                pl.ds(pl.multiple_of((ib % 2) * 256 + (ia // 4) * 128, 128), 128),
            ][:44]
            m = ps[8 * ib + ia].astype(F32) + upd
            mid[8 * ib + ia] = m
            c = m - jnp.mean(m, axis=-1, keepdims=True)
            n = c * lax.rsqrt(jnp.mean(c * c, axis=-1, keepdims=True) + 1e-05)
            pn[ia, 44 * ib : 44 * ib + 44] = n
        pn[ia, 484:512] = jnp.zeros((28, 128), F32)
        p = pn[ia].astype(BF)
        proj = lax.dot_general(wedge[...], p, NT, preferred_element_type=F32)
        left = sigmoid(proj[0:128]) * proj[128:256]
        right = sigmoid(proj[256:384]) * proj[384:512]
        rows = pl.ds(pl.multiple_of(ia * 128, 128), 128)
        for t in range(4):
            el[t, rows, :] = left[:, t * 128 : t * 128 + 128]
            er[t, rows, :] = right[:, t * 128 : t * 128 + 128]
        gate[ia] = sigmoid(jnp.dot(p, wgate[...], preferred_element_type=F32))
        return 0

    lax.fori_loop(0, 8, normalize, 0)

    def pack(c, _):
        for side, e in ((0, el), (32, er)):
            send[c, side : side + 32] = jnp.concatenate(
                [e[t, pl.ds(c, 8, stride=128), :] for t in range(4)], axis=0
            ).astype(BF)
        return 0

    lax.fori_loop(0, 128, pack, 0)


def triangle_kernel(send, out, rbuf, sb, s_ref, perm, lh, rh, lop, rop, lhs2, ob, ss, rsem, ls, ss2, rsem2):
    me = lax.axis_index("row") * COLS + lax.axis_index("col")
    sem = pltpu.get_barrier_semaphore()

    def greet(s, _):
        pl.semaphore_signal(sem, inc=1, device_id=dev((me + s) % N), device_id_type=MESH)
        return 0

    lax.fori_loop(1, N, greet, 0)
    pl.semaphore_wait(sem, N - 1)
    keep = pltpu.make_async_copy(send.at[me], rbuf.at[me], ls)
    keep.start()

    def scatter(s, _):
        t = mixed(me, s)
        pltpu.make_async_remote_copy(
            src_ref=send.at[t], dst_ref=rbuf.at[me], send_sem=ss, recv_sem=rsem, device_id=dev(t), device_id_type=MESH
        ).start()
        return 0

    lax.fori_loop(1, N, scatter, 0)

    def spread(b, _):
        f, n = iota((1024, 128), 0), iota((1024, 128), 1)
        k = n % 64
        hit = (f // 512 == n // 64) & (f % 512 == 44 * b + k) & (k < 44)
        s_ref[:, pl.ds(pl.multiple_of(b * 128, 128), 128)] = hit.astype(F32).astype(BF)
        return 0

    lax.fori_loop(0, 11, spread, 0)

    def columns(t, _):
        m, n = iota((704, 128), 0), iota((704, 128), 1) + t * 128
        j = 88 * ((m // 8) % 8) + 8 * (m // 64) + m % 8
        hit = (j == 44 * (n // 64) + n % 64) & (n % 64 < 44)
        perm[:, pl.ds(pl.multiple_of(t * 128, 128), 128)] = hit.astype(F32).astype(BF)
        return 0

    lax.fori_loop(0, 8, columns, 0)
    keep.wait()
    whole = pltpu.make_async_remote_copy(
        src_ref=send.at[pl.ds(0, N - 1)], dst_ref=rbuf.at[pl.ds(0, N - 1)], send_sem=ss, recv_sem=rsem,
        device_id=dev((me + 1) % N), device_id_type=MESH,
    )
    whole.wait_recv()

    def unpack(s, _):
        r, cc = s // COLS, s % COLS
        msg = rbuf[s].astype(F32)
        rows = pl.ds(pl.multiple_of((cc // 2) * 64 + r * 8, 8), 8)
        for t in range(4):
            lanes = pl.ds(pl.multiple_of((cc % 2) * 512 + t * 128, 128), 128)
            lh[rows, lanes] = msg[t * 8 : t * 8 + 8]
            rh[rows, lanes] = msg[32 + t * 8 : 40 + t * 8]
        return 0

    lax.fori_loop(0, N, unpack, 0)

    for src, dst in ((lh, lop), (rh, rop)):
        m = src[...].astype(BF)

        def widen(b, _, m=m, dst=dst):
            x = jnp.dot(m, s_ref[:, pl.ds(pl.multiple_of(b * 128, 128), 128)], preferred_element_type=F32).astype(BF)
            for p in range(8):
                dst[pl.ds(pl.multiple_of(b * 64, 64), 64), p * 128 : p * 128 + 128] = x[p * 64 : p * 64 + 64]
            return 0

        lax.fori_loop(0, 11, widen, 0)

    def product(b, _):
        rows = pl.ds(pl.multiple_of(b * 64, 64), 64)
        c = lax.dot_general(lop[rows, :], rop[...], NT, preferred_element_type=F32).astype(BF)
        d = jnp.dot(c, perm[...], preferred_element_type=F32).astype(BF)
        for p in range(8):
            lhs2[p * 64 : p * 64 + 64, pl.ds(pl.multiple_of(b * 128, 128), 128)] = d[:, p * 128 : p * 128 + 128]
        return 0

    lax.fori_loop(0, 11, product, 0)
    ob[...] = lax.dot_general(lhs2[...], s_ref[...], NT, preferred_element_type=F32)

    def repack(s, _):
        r, cc = s // COLS, s % COLS
        rows = pl.ds(pl.multiple_of((cc // 2) * 64 + r * 8, 8), 8)
        sb[s] = jnp.concatenate(
            [ob[rows, pl.ds(pl.multiple_of((cc % 2) * 512 + t * 128, 128), 128)] for t in range(4)], axis=0
        ).astype(BF)
        return 0

    lax.fori_loop(0, N, repack, 0)
    back = pltpu.make_async_copy(sb.at[me], out.at[me], ls)
    back.start()

    def scatter_back(s, _):
        t = mixed(me, s)
        pltpu.make_async_remote_copy(
            src_ref=sb.at[t], dst_ref=out.at[me], send_sem=ss2, recv_sem=rsem2, device_id=dev(t), device_id_type=MESH
        ).start()
        return 0

    lax.fori_loop(1, N, scatter_back, 0)
    back.wait()
    whole.wait_send()
    whole2 = pltpu.make_async_remote_copy(
        src_ref=sb.at[pl.ds(0, N - 1)], dst_ref=out.at[pl.ds(0, N - 1)], send_sem=ss2, recv_sem=rsem2,
        device_id=dev((me + 1) % N), device_id_type=MESH,
    )
    whole2.wait_recv()
    whole2.wait_send()


def finish_kernel(recv, mid, gate, wo, out, rc, br):
    def unpack(c, _):
        x = recv[c].astype(F32)
        for t in range(4):
            rc[t, pl.ds(pl.multiple_of(c * 8, 8), 8), :] = x[t * 8 : t * 8 + 8]
        return 0

    lax.fori_loop(0, N, unpack, 0)

    def finish(ia, _):
        for t in range(4):
            z = rc[t, pl.ds(ia, 128, stride=8), :]
            c = z - jnp.mean(z, axis=0, keepdims=True)
            n = (c * lax.rsqrt(jnp.mean(c * c, axis=0, keepdims=True) + 1e-05)).astype(BF)
            branch = lax.dot_general(n, wo[...], TN, preferred_element_type=F32)
            br[t * 128 : t * 128 + 128] = branch * gate[ia, t * 128 : t * 128 + 128]
        for ib in range(11):
            out[8 * ib + ia] = (mid[8 * ib + ia] + br[44 * ib : 44 * ib + 44]).astype(BF)
        return 0

    lax.fori_loop(0, 8, finish, 0)


def params(**kw):
    return pltpu.CompilerParams(vmem_limit_bytes=56 * 2**20, **kw)


def per_device(hf, ps, f1, f2, wo, wl, wr, wg, wout):
    eye = jnp.eye(4, dtype=BF)
    f1p = (eye[:, None, :, None] * f1[None, :, None, :]).reshape(1024, 128)
    f2r = f2.reshape(256, 4, 8).transpose(0, 2, 1)
    f2p = (eye[:, None, None, :, None] * f2r[None, :, :, None, :]).reshape(1024, 128)
    wt = wo.reshape(32, 32, 128).transpose(1, 0, 2).reshape(1024, 128)
    wedge = jnp.concatenate([wl, wr], axis=1).T
    dma = pltpu.SemaphoreType.DMA
    sds = jax.ShapeDtypeStruct
    lmsg, rmsg = pl.pallas_call(
        msa_kernel,
        out_shape=(sds((256, 768), BF), sds((256, 384), BF)),
        in_specs=[VM] * 3,
        out_specs=(VM, VM),
        scratch_shapes=[
            pltpu.VMEM((96, 1024), F32), pltpu.VMEM((128, 128), F32), pltpu.VMEM((16, 768), BF),
            pltpu.VMEM((2, 16, 384), BF), dma((16,)), dma((16,)), dma, dma,
        ],
        compiler_params=params(collective_id=0, has_side_effects=True),
    )(hf, f1p, f2p)
    send, mid, gate = pl.pallas_call(
        pair_kernel,
        out_shape=(sds((N, 64, 128), BF), sds((RI, CJ, 128), F32), sds((8, 512, 128), F32)),
        in_specs=[VM] * 6,
        out_specs=(VM, VM, VM),
        scratch_shapes=[
            pltpu.VMEM((384, 256), BF), pltpu.VMEM((4096, 512), BF), pltpu.VMEM((1152, 4096), BF),
            pltpu.VMEM((1152, 512), F32), pltpu.VMEM((8, 512, 128), F32), pltpu.VMEM((4, 1024, 128), F32),
            pltpu.VMEM((4, 1024, 128), F32),
        ],
        compiler_params=params(),
    )(lmsg, rmsg, ps, wt, wedge, wg)
    recv = pl.pallas_call(
        triangle_kernel,
        out_shape=sds((N, 32, 128), BF),
        in_specs=[VM],
        out_specs=VM,
        scratch_shapes=[
            pltpu.VMEM((N, 64, 128), BF), pltpu.VMEM((N, 32, 128), BF), pltpu.VMEM((1024, 1408), BF),
            pltpu.VMEM((704, 1024), BF), pltpu.VMEM((512, 1024), F32), pltpu.VMEM((512, 1024), F32),
            pltpu.VMEM((704, 1024), BF), pltpu.VMEM((704, 1024), BF), pltpu.VMEM((512, 1408), BF),
            pltpu.VMEM((512, 1024), F32), dma, dma, dma, dma, dma,
        ],
        compiler_params=params(collective_id=1, has_side_effects=True),
    )(send)
    return pl.pallas_call(
        finish_kernel,
        out_shape=sds((RI, CJ, 128), BF),
        in_specs=[VM] * 4,
        out_specs=VM,
        scratch_shapes=[pltpu.VMEM((4, 1024, 128), F32), pltpu.VMEM((512, 128), F32)],
        compiler_params=params(),
    )(recv, mid, gate, wout)


def solution(mesh):
    return jax.shard_map(
        per_device,
        mesh=mesh,
        in_specs=(P("col", "row", None), P("row", "col", None), P(), P(), P(), P(), P(), P(), P()),
        out_specs=P("row", "col", None),
        check_vma=False,
    )
```

time: 721 us -> 158 us (0.22)
  waiting for transfers between devices: 383 us -> 0 us
  local copies, waits for them, and re-layouts: 178 us -> 8.81 us
  Pallas kernels: 0 us -> 147 us
  matrix products: 75.4 us -> 0 us
  blocking collectives: 40.2 us -> 0 us
  other arithmetic: 20.9 us -> 1.71 us
  between operations: 13.3 us -> 0.07 us
  loops' own time: 7.21 us -> 0 us
    psum x2 -> x0, waiting for transfers between devices: 241 us -> none  [spread(): return lax.psum(jnp.where(mine, shard, jnp.zeros_like(shard)), axis)]
    pallas_call x0 -> x4, Pallas kernels: none -> 147 us  [the longest x1 87.7 us: per_device(): pl.pallas_call(triangle_kernel, out_shape=sds((N, 32, 128), BF), in_specs...]
    all_gather x2 -> x0, waiting for transfers between devices: 141 us -> none  [the longest x1 88.3 us: per_device(): edge_gathered = lax.all_gather(right_edge, 'col', axis=2, tiled=True)]
    dot_general x29 -> x0, matrix products: 75.4 us -> none  [the longest x11 32.1 us: outer_block(): jnp.einsum('rhp,rmw->hmpw', left_block_slice, seq_right, preferred_elemen...]
    convert_element_type x11 -> x0, local copies, waits for them, and re-layouts: 70.8 us -> none  [outer_block(): flat = outer_sum.astype(jnp.bfloat16).reshape(block_slice, col_count, -1)]
    all_gather x2 -> x0, blocking collectives: 40.2 us -> none  [the longest x1 22.5 us: per_device(): lax.all_gather(right_alignment, 'col', axis=0, tiled=True)]
    reshape x11 -> x1, local copies, waits for them, and re-layouts: 40.9 us -> 0.81 us  [per_device(): wt = wo.reshape(32, 32, 128).transpose(1, 0, 2).reshape(1024, 128)]
    all_gather x1 -> x0, local copies, waits for them, and re-layouts: 27.3 us -> none  [per_device(): lax.all_gather(left_edge, 'col', axis=2, tiled=True)]
  transfers between devices with their start and end apart: 4 -> 0, of which waited for: 4 -> 0; matrix products, arithmetic and copies ran while one was open for 9% -> 0% of each run, Pallas kernels for 0% -> 0%
where the time goes in v1:
time: 158 us
  Pallas kernels  147 us (93%)
  local copies, waits for them, and re-layouts  8.81 us (6%)
  other arithmetic  1.71 us (1%)
    pallas_call x1, Pallas kernels, per_device(): pl.pallas_call(triangle_kernel, out_shape=sds((N, 32, 128), BF), in_specs...  87.7 us
    pallas_call x1, Pallas kernels, per_device(): pl.pallas_call(pair_kernel, out_shape=(sds((N, 64, 128), BF), sds((RI, CJ...  29 us
    pallas_call x1, Pallas kernels, per_device(): pl.pallas_call(msa_kernel, out_shape=(sds((256, 768), BF), sds((256, 384)...  23.3 us
    pallas_call x1, Pallas kernels, per_device(): pl.pallas_call(finish_kernel, out_shape=sds((RI, CJ, 128), BF), in_specs=...  7.04 us

profile of v1, /device:TPU:1, one launch (start us, length us, event | category | flops | bytes accessed | tf_op | source)
XLA Modules:
  0.0 157.7 jit_solution(8009971805061914377)
XLA Ops:
  0.0 0.0 copy-start.1
  0.0 0.8 copy.17
  0.8 0.9 copy.21
  1.7 1.0 copy.22
  2.7 0.0 copy-start
  2.7 0.7 maximum_bitcast_fusion.wedge
  3.4 0.2 broadcast_multiply_fusion
  3.6 0.8 copy.19.f2p
  4.4 0.9 broadcast_multiply_fusion.1
  5.3 0.8 copy.18.f1p
  6.2 23.3 %shard_map.91 = (bf16[256,768]{1,0:T(8,128)(2,1)}, bf16[256,384]{1,0:T(8,128)(2,1)}) custom-call(bf16[4,88,256]{2,1,0:T(8,128)(2,1)} %hf.1, bf16[1024,128]{1,0:T(8,128)(2,1)} %copy.18.f1p, bf16[1024,128]{1,0:T(8,128)(2,1)} %copy.19.f2p), custom_call_target="tpu_custom_call" | custom-call | tf_op jit(solution)/shard_map/pallas_call | solution.py:359
  29.5 0.0 copy-done.1
  29.5 0.8 copy.20
  30.3 0.0 copy-done
  30.3 1.2 copy.23.ps
  31.5 29.0 %shard_map.92 = (bf16[128,64,128]{2,1,0:T(8,128)(2,1)}, f32[88,44,128]{2,1,0:T(8,128)}, f32[8,512,128]{2,1,0:T(8,128)}) custom-call(bf16[256,768]{1,0:T(8,128)(2,1)} %get-tuple-element.10.lmsg, bf16[256,384]{1,0:T(8,128)(2,1)} %get-tuple-element.11.rmsg, bf16[88,44,128]{2,1,0:T(8,128)(2,1)} %copy.23.ps, bf16[1024,128]{1,0:T(8,128)(2,1)} %bitcast.23, ...), custom_call_target="tpu_custom_call" | custom-call | tf_op jit(solution)/shard_map/pallas_call | solution.py:370
  60.5 87.7 %shard_map.93.recv = bf16[128,32,128]{2,1,0:T(8,128)(2,1)} custom-call(bf16[128,64,128]{2,1,0:T(8,128)(2,1)} %get-tuple-element.12.send), custom_call_target="tpu_custom_call" | custom-call | tf_op jit(solution)/shard_map/pallas_call | solution.py:382
  148.2 7.0 %shard_map.94 = bf16[88,44,128]{2,1,0:T(8,128)(2,1)} custom-call(bf16[128,32,128]{2,1,0:T(8,128)(2,1)} %shard_map.93.recv, f32[88,44,128]{2,1,0:T(8,128)} %get-tuple-element.13.mid, f32[8,512,128]{2,1,0:T(8,128)} %get-tuple-element.14.gate, bf16[128,128]{1,0:T(8,128)(2,1)} %wo.1), custom_call_target="tpu_custom_call" | custom-call | tf_op jit(solution)/shard_map/pallas_call | solution.py:395
  155.3 2.4 %copy.24 = bf16[88,44,128]{2,0,1:T(8,128)(2,1)} copy(bf16[88,44,128]{2,1,0:T(8,128)(2,1)} %shard_map.94) | data formatting | bytes 1982464 | tf_op jit(solution)/shard_map/pallas_call | solution.py:395
  (3 shorter events, 0.1 us)
Async XLA Ops:
  0.0 29.5 %copy-start.1 = (bf16[1024,128]{1,0:T(8,128)(2,1)S(1)}, bf16[1024,128]{1,0:T(8,128)(2,1)}, u32[]{:S(2)}) copy-start(bf16[1024,128]{1,0:T(8,128)(2,1)} %param.13) | copy-start | bytes 786436
  2.7 27.6 %copy-start = (bf16[88,44,128]{2,0,1:T(8,128)(2,1)S(1)}, bf16[88,44,128]{2,0,1:T(8,128)(2,1)}, u32[]{:S(2)}) copy-start(bf16[88,44,128]{2,0,1:T(8,128)(2,1)} %param.10) | copy-start | bytes 2973700

commit v2 on v0

v2 whole, which is shorter than its diff:
```python
import jax
import jax.numpy as jnp
from jax import lax
from jax.experimental import pallas as pl
from jax.experimental.pallas import tpu as pltpu
from jax.sharding import PartitionSpec as P

ROWS, COLS = 8, 16
N = ROWS * COLS
RI, CJ = 88, 44
PITCH, PITCH2 = 136, 24
MESH = pl.DeviceIdType.MESH
VM = pl.BlockSpec(memory_space=pltpu.VMEM)
F32, BF = jnp.float32, jnp.bfloat16
NT = (((1,), (1,)), ((), ()))
TN = (((0,), (0,)), ((), ()))
SPAN = ((0, 3), (2, 6), (5, 9), (8, 11))


def dev(flat):
    return (flat // COLS, flat % COLS)


def shifted(me, a, b, c, dk):
    row, col = me // COLS, me % COLS
    x, y, z, k = col // 4, (row // 4) * 2 + (col // 2) % 2, row % 4, col % 2
    x, y, z, k = (x + a) % 4, (y + b) % 4, (z + c) % 4, (k + dk) % 2
    return ((y // 2) * 4 + z) * COLS + x * 4 + (y % 2) * 2 + k


def mixed(me, step):
    u = (step * 37) % 128
    a, b, c, dk = u % 4, (u // 4) % 4, (u // 16) % 4, u // 64
    return shifted(me, a, a + b, a + c, dk)


def sigmoid(v):
    return 0.5 * jnp.tanh(0.5 * v) + 0.5


def iota(shape, dim):
    return lax.broadcasted_iota(jnp.int32, shape, dim)


def ones_where(mask):
    return mask.astype(F32).astype(BF)


def at(start, size, align):
    return pl.ds(pl.multiple_of(start, align), size)


def kernel(
    hf, ps, f1, f2, wo, wl, wr, wg, wout, out,
    a_ref, p_ref, ls, rs32, rs, lmsg, rt, rmsg, rmt, wof, bd, lhs, osc, psf, pn, el, er, wedge, gate,
    send, lh, sw, s2, lop, rop32, rop, lhs2, sb, rv, rc, br,
    l_send, l_recv, r1_send, r1_recv, r2_send, r2_recv, e_send, e_recv, c_send, c_recv,
):
    row, col = lax.axis_index("row"), lax.axis_index("col")
    me = row * COLS + col
    sem = pltpu.get_barrier_semaphore()

    def greet(s, _):
        pl.semaphore_signal(sem, inc=1, device_id=dev((me + s) % N), device_id_type=MESH)
        return 0

    lax.fori_loop(1, N, greet, 0)

    v = hf[...].astype(F32)
    centered = v - jnp.mean(v, axis=-1, keepdims=True)
    mn = centered * lax.rsqrt(jnp.mean(centered * centered, axis=-1, keepdims=True) + 1e-05)
    for s in range(4):
        for g in range(22):
            qt, q = g // 4, g % 4
            a_ref[qt * 16 + s * 4 : qt * 16 + s * 4 + 4, q * 256 : q * 256 + 256] = mn[s, g * 4 : g * 4 + 4]
    a_ref[80:96, 512:1024] = jnp.zeros((16, 512), F32)
    lm = jnp.concatenate(
        [
            jnp.dot(a_ref[:, q * 256 : q * 256 + 256].astype(BF), f1[...], preferred_element_type=F32)
            for q in range(4)
        ],
        axis=1,
    )
    for qt in range(6):
        ls[:, qt * 128 : qt * 128 + 128] = lm[qt * 16 : qt * 16 + 16].astype(BF)
    pr = jnp.concatenate(
        [jnp.dot(mn[s].astype(BF), f2[...], preferred_element_type=F32) for s in range(4)], axis=1
    )
    p_ref[...] = jnp.zeros(p_ref.shape, F32)
    p_ref[0:44] = pr[0:44]
    p_ref[64:108] = pr[44:88]
    tr = p_ref[...].T
    for h in range(2):
        for s in range(4):
            rs32[h, s * 4 : s * 4 + 4, :] = jnp.concatenate(
                [tr[s * 32 + eg * 4 : s * 32 + eg * 4 + 4, h * 64 : h * 64 + 48] for eg in range(8)], axis=1
            )
    rs[...] = rs32[...].astype(BF)
    pl.semaphore_wait(sem, N - 1)

    own = at(col * 16, 16, 16)
    pltpu.make_async_copy(ls, lmsg.at[own], l_recv).start()
    pltpu.make_async_copy(rs, rt.at[row], r1_recv).start()

    def send_right(s, _):
        pltpu.make_async_remote_copy(
            src_ref=rs, dst_ref=rt.at[row], send_sem=r1_send, recv_sem=r1_recv,
            device_id=((row + s) % ROWS, col), device_id_type=MESH,
        ).start()
        return 0

    lax.fori_loop(1, ROWS, send_right, 0)

    def send_left(s, _):
        pltpu.make_async_remote_copy(
            src_ref=ls, dst_ref=lmsg.at[own], send_sem=l_send, recv_sem=l_recv,
            device_id=(row, (col + s) % COLS), device_id_type=MESH,
        ).start()
        return 0

    lax.fori_loop(1, COLS, send_left, 0)

    wof[...] = wo[...].astype(F32)
    bd[...] = jnp.zeros(bd.shape, BF)

    def place(b, _):
        w = wof[pl.ds((b % 8) * 4 + b // 8, 32, stride=32), :].astype(BF)
        for q in range(4):
            bd[at(b * 128 + q * 32, 32, 32), q * 128 : q * 128 + 128] = w
        return 0

    lax.fori_loop(0, 32, place, 0, unroll=4)
    pltpu.make_async_copy(rt, rt, r1_recv).wait()
    own_half = pltpu.make_async_copy(rt.at[col // 2, col % 2], rmsg.at[own], r2_recv)
    own_half.start()

    def forward_right(s, _):
        t = (col + s) % COLS
        pltpu.make_async_remote_copy(
            src_ref=rt.at[t // 2, t % 2], dst_ref=rmsg.at[own], send_sem=r2_send, recv_sem=r2_recv,
            device_id=(row, t), device_id_type=MESH,
        ).start()
        return 0

    lax.fori_loop(1, COLS, forward_right, 0)
    psf[...] = ps[...].reshape(CJ * RI, 128).astype(F32)
    wedge[0:256] = wl[...].T
    wedge[256:512] = wr[...].T
    pltpu.make_async_copy(rmsg, rmsg, r2_recv).wait()
    pltpu.make_async_copy(lmsg, lmsg, l_recv).wait()

    rmt[...] = rmsg[...].T

    def outer(u, _):
        a, b = iota((256, 256), 0), iota((256, 256), 1)
        for w in range(4):
            pick = ones_where((a // 4 == b // 4) & (a % 4 == w) & (b % 4 == u))
            sel = jnp.dot(rmt[...], pick, preferred_element_type=F32).astype(BF)
            x = jnp.dot(sel, lmsg[...], preferred_element_type=F32) * (1.0 / 64)
            for eg in range(8):
                for qt in range(6):
                    lhs[at(u * 288 + qt * 48, 48, 16), w * 1024 + eg * 128 : w * 1024 + eg * 128 + 128] = x[
                        eg * 48 : eg * 48 + 48, qt * 128 : qt * 128 + 128
                    ].astype(BF)
        return 0

    lax.fori_loop(0, 4, outer, 0)

    def project(u, _):
        rows = at(u * 288, 288, 16)
        osc[rows, :] = jnp.dot(lhs[rows, :], bd[...], preferred_element_type=F32)
        return 0

    lax.fori_loop(0, 4, project, 0)

    for half in range(2):
        lo, hi = (0, 6) if half == 0 else (6, 11)

        def normalize(ia, _, lo=lo, hi=hi, half=half):
            for ib in range(lo, hi):
                i = 11 * ia + ib
                upd = osc[at((i % 4) * 288 + (i // 16) * 48, 48, 8), at((i % 16) // 4 * 128, 128, 128)][:44]
                cells = pl.ds(i, CJ, stride=RI)
                m = psf[cells, :] + upd
                psf[cells, :] = m
                c = m - jnp.mean(m, axis=-1, keepdims=True)
                n = c * lax.rsqrt(jnp.mean(c * c, axis=-1, keepdims=True) + 1e-05)
                pn[ia, 44 * ib : 44 * ib + 44] = n
            if half:
                pn[ia, 484:512] = jnp.zeros((28, 128), F32)
            p = pn[ia, half * 256 : half * 256 + 256].astype(BF)
            proj = lax.dot_general(wedge[...], p, NT, preferred_element_type=F32)
            left = sigmoid(proj[0:128]) * proj[128:256]
            right = sigmoid(proj[256:384]) * proj[384:512]
            rows = at(ia * PITCH, 128, 8)
            for t in range(2):
                el[t, rows, :] = left[:, t * 128 : t * 128 + 128]
                er[t, rows, :] = right[:, t * 128 : t * 128 + 128]
            return 0

        lax.fori_loop(0, 8, normalize, 0)

        def pack(c, _, half=half):
            for t in range(2):
                cells = pl.ds(c, 8, stride=PITCH)
                send[c, 2 * half + t] = jnp.concatenate([el[t, cells, :], er[t, cells, :]], axis=0).astype(BF)
            return 0

        lax.fori_loop(0, N, pack, 0, unroll=8)
        cells = lh.at[2 * half : 2 * half + 2, at(((col // 2) * 8 + row) * 16, 16, 16), at(col % 2 * 128, 128, 128)]
        pltpu.make_async_copy(send.at[me, 2 * half : 2 * half + 2], cells, e_recv.at[half]).start()

        def scatter(s, _, half=half, cells=cells):
            t = mixed(me, s)
            pltpu.make_async_remote_copy(
                src_ref=send.at[t, 2 * half : 2 * half + 2], dst_ref=cells, send_sem=e_send.at[half],
                recv_sem=e_recv.at[half], device_id=dev(t), device_id_type=MESH,
            ).start()
            return 0

        lax.fori_loop(1, N, scatter, 0)

    for t in range(4):
        lo, hi = SPAN[t]
        for b in range(lo, hi):
            f, n = iota((256, 128), 0), iota((256, 128), 1)
            k = n % 64
            hit = (f // 128 == n // 64) & (f % 128 + 128 * t == 44 * b + k) & (k < 44)
            sw[t, :, (b - lo) * 128 : (b - lo) * 128 + 128] = ones_where(hit)
            n, f = iota((128, 256), 0), iota((128, 256), 1)
            k = n % 16
            hit = (f // 128 == n // 64) & (f % 128 + 128 * t == 44 * b + 11 * (n % 64 // 16) + k) & (k < 11)
            s2[t, (b - lo) * 128 : (b - lo) * 128 + 128, :] = ones_where(hit)
    rop32[...] = jnp.zeros(rop32.shape, F32)

    def gates(ia, _):
        gate[ia] = sigmoid(jnp.dot(pn[ia].astype(BF), wg[...], preferred_element_type=F32))
        return 0

    lax.fori_loop(0, 8, gates, 0)

    for half in range(2):
        part = lh.at[2 * half : 2 * half + 2]
        pltpu.make_async_copy(part, part, e_recv.at[half]).wait()

    def widen(m, _):
        ys = []
        for t in range(4):
            lo, hi = SPAN[t]
            ys.append(
                jnp.dot(lh[t, at(m * 256, 256, 256), :], sw[t, :, : (hi - lo) * 128], preferred_element_type=F32)
            )
        for b in range(11):
            x = None
            for t in range(4):
                lo, hi = SPAN[t]
                if lo <= b < hi:
                    y = ys[t][:, (b - lo) * 128 : (b - lo) * 128 + 128]
                    x = y if x is None else x + y
            x = x.reshape(2, 8, 2, 8, 128)
            for q in range(2):
                p = 2 * m + q
                lop[b * 64 : b * 64 + 64, at(p * 128, 128, 128)] = x[q, :, 0].reshape(64, 128).astype(BF)
                for r in range(8):
                    rop32[p, pl.ds(r * 128 + b, 8, stride=16), :] = x[q, r, 1]
        return 0

    lax.fori_loop(0, 4, widen, 0)
    for p in range(8):
        rop[:, p * 128 : p * 128 + 128] = rop32[p].astype(BF)

    x0 = col // 4

    def product(step, _):
        dx = (step + 2) % 4
        g = (x0 + dx) % 4
        c = lax.dot_general(lop[...], rop[at(g * 256, 256, 256), :], NT, preferred_element_type=F32).astype(BF)
        for q in range(2):
            for b in range(11):
                lhs2[q * 64 : q * 64 + 64, b * 128 : b * 128 + 128] = c[b * 64 : b * 64 + 64, q * 128 : q * 128 + 128]
        zs = []
        for t in range(4):
            lo, hi = SPAN[t]
            z = jnp.dot(lhs2[:, lo * 128 : hi * 128], s2[t, : (hi - lo) * 128, :], preferred_element_type=F32)
            zs.append(z.reshape(16, 8, 256))
        for h in range(2):
            z = jnp.concatenate([zs[2 * h], zs[2 * h + 1]], axis=1).astype(BF)
            sb[h, at(g * 16, 16, 16)] = z

        def scatter_back(s, _):
            u = (s * 5 + step) % 32
            t = shifted(me, dx, u % 4, (u // 4 + u) % 4, u // 16)
            r, cc = t // COLS, t % COLS

            @pl.when(t != me)
            def _():
                pltpu.make_async_remote_copy(
                    src_ref=sb.at[:, cc // 2 * 8 + r, :, at(cc % 2 * 128, 128, 128)], dst_ref=rv.at[me],
                    send_sem=c_send, recv_sem=c_recv, device_id=dev(t), device_id_type=MESH,
                ).start()

            return 0

        lax.fori_loop(0, 32, scatter_back, 0)
        return 0

    lax.fori_loop(0, 4, product, 0)
    back = sb.at[:, col // 2 * 8 + row, :, at(col % 2 * 128, 128, 128)]
    pltpu.make_async_copy(back, rv.at[me], c_recv).start()
    pltpu.make_async_copy(rv, rv, c_recv).wait()

    def unpack(c, _):
        for h in range(2):
            rc[h, at(c * PITCH2, 16, 8), :] = rv[c, h].astype(F32)
        return 0

    lax.fori_loop(0, N, unpack, 0, unroll=8)

    def finish(ia, _):
        for t in range(4):
            z = rc[t // 2, pl.ds(t % 2 * 8 + ia, 128, stride=PITCH2), :]
            c = z - jnp.mean(z, axis=0, keepdims=True)
            n = (c * lax.rsqrt(jnp.mean(c * c, axis=0, keepdims=True) + 1e-05)).astype(BF)
            branch = lax.dot_general(n, wout[...], TN, preferred_element_type=F32)
            br[t * 128 : t * 128 + 128] = branch * gate[ia, t * 128 : t * 128 + 128]
        for ib in range(11):
            cells = pl.ds(11 * ia + ib, CJ, stride=RI)
            psf[cells, :] = psf[cells, :] + br[44 * ib : 44 * ib + 44]
        return 0

    lax.fori_loop(0, 8, finish, 0)
    out[...] = psf[...].astype(BF).reshape(CJ, RI, 128)

    def sent(src, sem):
        pltpu.make_async_remote_copy(
            src_ref=src, dst_ref=src, send_sem=sem, recv_sem=l_recv, device_id=dev((me + 1) % N), device_id_type=MESH
        ).wait_send()

    sent(lmsg.at[0:240], l_send)
    sent(rt.at[0:7], r1_send)
    sent(rmsg.at[0:240], r2_send)
    for half in range(2):
        sent(send.at[0 : N - 1, 0:2], e_send.at[half])
    sent(rv.at[0 : N - 1], c_send)


def per_device(hf, ps, f1, f2, wo, wl, wr, wg, wout):
    dma = pltpu.SemaphoreType.DMA
    vm = pltpu.VMEM
    out = pl.pallas_call(
        kernel,
        out_shape=jax.ShapeDtypeStruct((CJ, RI, 128), BF),
        in_specs=[VM] * 9,
        out_specs=VM,
        scratch_shapes=[
            vm((96, 1024), F32), vm((128, 128), F32), vm((16, 768), BF), vm((2, 16, 384), F32), vm((2, 16, 384), BF),
            vm((256, 768), BF), vm((8, 2, 16, 384), BF), vm((256, 384), BF), vm((384, 256), BF), vm((1024, 128), F32),
            vm((4096, 512), BF), vm((1152, 4096), BF), vm((1152, 512), F32), vm((CJ * RI, 128), F32),
            vm((8, 512, 128), F32), vm((2, 8 * PITCH, 128), F32), vm((2, 8 * PITCH, 128), F32), vm((512, 128), BF),
            vm((8, 512, 128), F32), vm((N, 4, 16, 128), BF), vm((4, 1024, 256), BF), vm((4, 256, 512), BF),
            vm((4, 512, 256), BF), vm((704, 1024), BF), vm((8, 1024, 128), F32), vm((1024, 1024), BF),
            vm((128, 1408), BF), vm((2, 64, 16, 256), BF), vm((N, 2, 16, 128), BF), vm((2, N * PITCH2, 128), F32),
            vm((512, 128), F32),
            dma, dma, dma, dma, dma, dma, dma((2,)), dma((2,)), dma, dma,
        ],
        compiler_params=pltpu.CompilerParams(
            vmem_limit_bytes=60 * 2**20, collective_id=0, has_side_effects=True
        ),
    )(hf, ps.transpose(1, 0, 2), f1, f2, wo, wl, wr, wg, wout)
    return out.transpose(1, 0, 2)


def solution(mesh):
    return jax.shard_map(
        per_device,
        mesh=mesh,
        in_specs=(P("col", "row", None), P("row", "col", None), P(), P(), P(), P(), P(), P(), P()),
        out_specs=P("row", "col", None),
        check_vma=False,
    )
```

time: 721 us -> 103 us (0.14)
  waiting for transfers between devices: 383 us -> 0 us
  local copies, waits for them, and re-layouts: 178 us -> 4.41 us
  Pallas kernels: 0 us -> 98.3 us
  matrix products: 75.4 us -> 0 us
  blocking collectives: 40.2 us -> 0 us
  other arithmetic: 20.9 us -> 0 us
  between operations: 13.3 us -> 0.01 us
  loops' own time: 7.21 us -> 0 us
    psum x2 -> x0, waiting for transfers between devices: 241 us -> none  [spread(): return lax.psum(jnp.where(mine, shard, jnp.zeros_like(shard)), axis)]
    all_gather x2 -> x0, waiting for transfers between devices: 141 us -> none  [the longest x1 88.3 us: per_device(): edge_gathered = lax.all_gather(right_edge, 'col', axis=2, tiled=True)]
    pallas_call x0 -> x1, Pallas kernels: none -> 98.3 us  [per_device(): pl.pallas_call(kernel, out_shape=jax.ShapeDtypeStruct((CJ, RI, 128), BF),...]
    dot_general x29 -> x0, matrix products: 75.4 us -> none  [the longest x11 32.1 us: outer_block(): jnp.einsum('rhp,rmw->hmpw', left_block_slice, seq_right, preferred_elemen...]
    convert_element_type x11 -> x0, local copies, waits for them, and re-layouts: 70.8 us -> none  [outer_block(): flat = outer_sum.astype(jnp.bfloat16).reshape(block_slice, col_count, -1)]
    reshape x11 -> x0, local copies, waits for them, and re-layouts: 40.9 us -> none  [outer_block(): flat = outer_sum.astype(jnp.bfloat16).reshape(block_slice, col_count, -1)]
    all_gather x2 -> x0, blocking collectives: 40.2 us -> none  [the longest x1 22.5 us: per_device(): lax.all_gather(right_alignment, 'col', axis=0, tiled=True)]
    all_gather x1 -> x0, local copies, waits for them, and re-layouts: 27.3 us -> none  [per_device(): lax.all_gather(left_edge, 'col', axis=2, tiled=True)]
  transfers between devices with their start and end apart: 4 -> 0, of which waited for: 4 -> 0; matrix products, arithmetic and copies ran while one was open for 9% -> 0% of each run, Pallas kernels for 0% -> 0%
where the time goes in v2:
time: 103 us
  Pallas kernels  98.3 us (95%)
  local copies, waits for them, and re-layouts  4.41 us (4%)
    pallas_call x1, Pallas kernels, per_device(): pl.pallas_call(kernel, out_shape=jax.ShapeDtypeStruct((CJ, RI, 128), BF),...  98.3 us
    unnamed x5, local copies, waits for them, and re-layouts  4.41 us

profile of v2, /device:TPU:1, one launch (start us, length us, event | category | flops | bytes accessed | tf_op | source)
XLA Modules:
  0.0 102.7 jit_solution(7557317231239595346)
XLA Ops:
  0.0 0.0 copy-start
  0.0 1.5 %copy.10.f1 = bf16[256,32]{1,0:T(8,128)(2,1)} copy(bf16[256,32]{0,1:T(8,128)(2,1)} %param.11) | data formatting | bytes 32768 | tf_op args[2]
  1.5 0.0 copy-done
  1.5 0.7 copy.11.f2
  2.2 98.3 %shard_map.91 = bf16[44,88,128]{2,1,0:T(8,128)(2,1)} custom-call(bf16[4,88,256]{2,1,0:T(8,128)(2,1)} %hf.1, bf16[44,88,128]{2,1,0:T(8,128)(2,1)} %bitcast.3, bf16[256,32]{1,0:T(8,128)(2,1)} %copy.10.f1, bf16[256,32]{1,0:T(8,128)(2,1)} %copy.11.f2, bf16[1024,128]{1,0:T(8,128)(2,1)} %wo.1, bf16[128,256]{1,0:T(8,128)(2,1)} %wl.1, bf16[128,256]{1,0:T(8,128)(2,1)} %wr.1, ...), custom_call_target="tpu_custom_call" | custom-call | tf_op jit(solution)/shard_map/pallas_call | solution.py:350
  100.5 2.2 %copy.13 = bf16[88,44,128]{2,0,1:T(8,128)(2,1)} copy(bf16[88,44,128]{2,0,1:T(8,128)(2,1)} %bitcast.2) | data formatting | bytes 1982464
Async XLA Ops:
  0.0 1.5 %copy-start = (bf16[256,32]{0,1:T(8,128)(2,1)S(1)}, bf16[256,32]{0,1:T(8,128)(2,1)}, u32[]{:S(2)}) copy-start(bf16[256,32]{0,1:T(8,128)(2,1)} %param.12) | copy-start | bytes 49156

commit v3 on v2

--- a/solution.py
+++ b/solution.py
@@ -17,21 +17,22 @@
 SPAN = ((0, 3), (2, 6), (5, 9), (8, 11))
 
 
+def in_half(a, b):
+    return 6 * a + b if b < 6 else 24 + 5 * a + b - 6
+
+
+def slot(ia, ib):
+    i = in_half(ia % 4, ib)
+    first = i // 4 if ib < 6 else i // 4 + 6
+    return first + (ia // 4) * (6 if ib < 6 else 5), i % 4
+
+
+def group_rows(g):
+    return 4 * (g if g < 6 else g + 5 if g < 12 else g - 6 if g < 17 else g)
+
+
 def dev(flat):
     return (flat // COLS, flat % COLS)
-
-
-def shifted(me, a, b, c, dk):
-    row, col = me // COLS, me % COLS
-    x, y, z, k = col // 4, (row // 4) * 2 + (col // 2) % 2, row % 4, col % 2
-    x, y, z, k = (x + a) % 4, (y + b) % 4, (z + c) % 4, (k + dk) % 2
-    return ((y // 2) * 4 + z) * COLS + x * 4 + (y % 2) * 2 + k
-
-
-def mixed(me, step):
-    u = (step * 37) % 128
-    a, b, c, dk = u % 4, (u // 4) % 4, (u // 16) % 4, u // 64
-    return shifted(me, a, a + b, a + c, dk)
 
 
 def sigmoid(v):
@@ -58,13 +59,27 @@
 ):
     row, col = lax.axis_index("row"), lax.axis_index("col")
     me = row * COLS + col
+    around = [lax.rem(col + c, COLS) for c in range(COLS)]
+    x, y = col // 4, row // 4 * 2 + col // 2 % 2
+    x_col = [lax.rem(x + d, 4) * 4 for d in range(4)]
+    y_col = [lax.rem(lax.rem(y + d, 4), 2) * 2 for d in range(4)]
+    y_row = [lax.div(lax.rem(y + d, 4), 2) * 4 for d in range(4)]
     sem = pltpu.get_barrier_semaphore()
 
-    def greet(s, _):
-        pl.semaphore_signal(sem, inc=1, device_id=dev((me + s) % N), device_id_type=MESH)
-        return 0
-
-    lax.fori_loop(1, N, greet, 0)
+    def greet(o, _):
+        r = lax.rem(row + o, ROWS)
+        for c in range(COLS):
+            if c:
+                pl.semaphore_signal(sem, inc=1, device_id=(r, around[c]), device_id_type=MESH)
+            else:
+
+                @pl.when(o > 0)
+                def _():
+                    pl.semaphore_signal(sem, inc=1, device_id=(r, col), device_id_type=MESH)
+
+        return 0
+
+    lax.fori_loop(0, ROWS, greet, 0)
 
     v = hf[...].astype(F32)
     centered = v - jnp.mean(v, axis=-1, keepdims=True)
@@ -72,11 +87,13 @@
     for s in range(4):
         for g in range(22):
             qt, q = g // 4, g % 4
-            a_ref[qt * 16 + s * 4 : qt * 16 + s * 4 + 4, q * 256 : q * 256 + 256] = mn[s, g * 4 : g * 4 + 4]
+            a_ref[qt * 16 + s * 4 : qt * 16 + s * 4 + 4, q * 256 : q * 256 + 256] = mn[
+                s, group_rows(g) : group_rows(g) + 4
+            ]
     a_ref[80:96, 512:1024] = jnp.zeros((16, 512), F32)
     lm = jnp.concatenate(
         [
-            jnp.dot(a_ref[:, q * 256 : q * 256 + 256].astype(BF), f1[...], preferred_element_type=F32)
+            lax.dot_general(a_ref[:, q * 256 : q * 256 + 256].astype(BF), f1[...], NT, preferred_element_type=F32)
             for q in range(4)
         ],
         axis=1,
@@ -84,7 +101,7 @@
     for qt in range(6):
         ls[:, qt * 128 : qt * 128 + 128] = lm[qt * 16 : qt * 16 + 16].astype(BF)
     pr = jnp.concatenate(
-        [jnp.dot(mn[s].astype(BF), f2[...], preferred_element_type=F32) for s in range(4)], axis=1
+        [lax.dot_general(mn[s].astype(BF), f2[...], NT, preferred_element_type=F32) for s in range(4)], axis=1
     )
     p_ref[...] = jnp.zeros(p_ref.shape, F32)
     p_ref[0:44] = pr[0:44]
@@ -105,7 +122,7 @@
     def send_right(s, _):
         pltpu.make_async_remote_copy(
             src_ref=rs, dst_ref=rt.at[row], send_sem=r1_send, recv_sem=r1_recv,
-            device_id=((row + s) % ROWS, col), device_id_type=MESH,
+            device_id=(lax.rem(row + s, ROWS), col), device_id_type=MESH,
         ).start()
         return 0
 
@@ -114,7 +131,7 @@
     def send_left(s, _):
         pltpu.make_async_remote_copy(
             src_ref=ls, dst_ref=lmsg.at[own], send_sem=l_send, recv_sem=l_recv,
-            device_id=(row, (col + s) % COLS), device_id_type=MESH,
+            device_id=(row, lax.rem(col + s, COLS)), device_id_type=MESH,
         ).start()
         return 0
 
@@ -135,9 +152,9 @@
     own_half.start()
 
     def forward_right(s, _):
-        t = (col + s) % COLS
+        t = lax.rem(col + s, COLS)
         pltpu.make_async_remote_copy(
-            src_ref=rt.at[t // 2, t % 2], dst_ref=rmsg.at[own], send_sem=r2_send, recv_sem=r2_recv,
+            src_ref=rt.at[lax.div(t, 2), lax.rem(t, 2)], dst_ref=rmsg.at[own], send_sem=r2_send, recv_sem=r2_recv,
             device_id=(row, t), device_id_type=MESH,
         ).start()
         return 0
@@ -159,28 +176,58 @@
             x = jnp.dot(sel, lmsg[...], preferred_element_type=F32) * (1.0 / 64)
             for eg in range(8):
                 for qt in range(6):
-                    lhs[at(u * 288 + qt * 48, 48, 16), w * 1024 + eg * 128 : w * 1024 + eg * 128 + 128] = x[
-                        eg * 48 : eg * 48 + 48, qt * 128 : qt * 128 + 128
-                    ].astype(BF)
+                    lhs[
+                        at(qt // 3 * 576 + u * 144 + qt % 3 * 48, 48, 16),
+                        w * 1024 + eg * 128 : w * 1024 + eg * 128 + 128,
+                    ] = x[eg * 48 : eg * 48 + 48, qt * 128 : qt * 128 + 128].astype(BF)
         return 0
 
     lax.fori_loop(0, 4, outer, 0)
 
-    def project(u, _):
-        rows = at(u * 288, 288, 16)
-        osc[rows, :] = jnp.dot(lhs[rows, :], bd[...], preferred_element_type=F32)
-        return 0
-
-    lax.fori_loop(0, 4, project, 0)
+    def cells_of(half):
+        rows = at(((col // 2) * 8 + row) * 16, 16, 16)
+        return lh.at[2 * half : 2 * half + 2, rows, at(col % 2 * 128, 128, 128)]
+
+    def scatter(half, o):
+        z_row = [lax.rem(row + o + d, 4) for d in range(4)]
+        k = lax.rem(col + lax.div(o, 4), 2)
+        for b in range(4):
+            for a in range(4):
+                r = y_row[(a + b) % 4] + z_row[a]
+                c = x_col[a] + y_col[(a + b) % 4] + k
+
+                def start(r=r, c=c):
+                    pltpu.make_async_remote_copy(
+                        src_ref=send.at[r * COLS + c, 2 * half : 2 * half + 2], dst_ref=cells_of(half),
+                        send_sem=e_send.at[half], recv_sem=e_recv.at[half], device_id=(r, c), device_id_type=MESH,
+                    ).start()
+
+                if a or b:
+                    start()
+                else:
+                    pl.when(o > 0)(start)
 
     for half in range(2):
         lo, hi = (0, 6) if half == 0 else (6, 11)
 
+        def project(u, _, half=half):
+            if half:
+                scatter(0, 2 * u)
+                scatter(0, 2 * u + 1)
+            rows = at(half * 576 + u * 288, 288, 16)
+            osc[at(u * 288, 288, 16), :] = jnp.dot(lhs[rows, :], bd[...], preferred_element_type=F32)
+            return 0
+
+        lax.fori_loop(0, 2, project, 0)
+
         def normalize(ia, _, lo=lo, hi=hi, half=half):
+            if half:
+                pl.when(lax.rem(ia, 2) == 0)(lambda: scatter(0, 4 + lax.div(ia, 2)))
             for ib in range(lo, hi):
-                i = 11 * ia + ib
-                upd = osc[at((i % 4) * 288 + (i // 16) * 48, 48, 8), at((i % 16) // 4 * 128, 128, 128)][:44]
-                cells = pl.ds(i, CJ, stride=RI)
+                g, u = slot(ia, ib)
+                g = g - 12 * half
+                upd = osc[at(u * 144 + g // 4 * 48, 48, 8), at(g % 4 * 128, 128, 128)][:44]
+                cells = pl.ds(44 * (ia // 4) + in_half(ia % 4, ib), CJ, stride=RI)
                 m = psf[cells, :] + upd
                 psf[cells, :] = m
                 c = m - jnp.mean(m, axis=-1, keepdims=True)
@@ -207,18 +254,13 @@
             return 0
 
         lax.fori_loop(0, N, pack, 0, unroll=8)
-        cells = lh.at[2 * half : 2 * half + 2, at(((col // 2) * 8 + row) * 16, 16, 16), at(col % 2 * 128, 128, 128)]
-        pltpu.make_async_copy(send.at[me, 2 * half : 2 * half + 2], cells, e_recv.at[half]).start()
-
-        def scatter(s, _, half=half, cells=cells):
-            t = mixed(me, s)
-            pltpu.make_async_remote_copy(
-                src_ref=send.at[t, 2 * half : 2 * half + 2], dst_ref=cells, send_sem=e_send.at[half],
-                recv_sem=e_recv.at[half], device_id=dev(t), device_id_type=MESH,
-            ).start()
-            return 0
-
-        lax.fori_loop(1, N, scatter, 0)
+        pltpu.make_async_copy(send.at[me, 2 * half : 2 * half + 2], cells_of(half), e_recv.at[half]).start()
+
+    def scatter_all(o, _):
+        scatter(1, o)
+        return 0
+
+    lax.fori_loop(0, 8, scatter_all, 0)
 
     for t in range(4):
         lo, hi = SPAN[t]
@@ -229,7 +271,8 @@
             sw[t, :, (b - lo) * 128 : (b - lo) * 128 + 128] = ones_where(hit)
             n, f = iota((128, 256), 0), iota((128, 256), 1)
             k = n % 16
-            hit = (f // 128 == n // 64) & (f % 128 + 128 * t == 44 * b + 11 * (n % 64 // 16) + k) & (k < 11)
+            j = jnp.where(k < 6, 6 * (n % 64 // 16) + k, 5 * (n % 64 // 16) + k + 18)
+            hit = (f // 128 == n // 64) & (f % 128 + 128 * t == 44 * b + j) & (k < 11)
             s2[t, (b - lo) * 128 : (b - lo) * 128 + 128, :] = ones_where(hit)
     rop32[...] = jnp.zeros(rop32.shape, F32)
 
@@ -269,12 +312,16 @@
     for p in range(8):
         rop[:, p * 128 : p * 128 + 128] = rop32[p].astype(BF)
 
-    x0 = col // 4
+    y0 = col // 2 % 2
 
     def product(step, _):
-        dx = (step + 2) % 4
-        g = (x0 + dx) % 4
-        c = lax.dot_general(lop[...], rop[at(g * 256, 256, 256), :], NT, preferred_element_type=F32).astype(BF)
+        odd, flip = step % 2, step // 2
+        pairs = (
+            2 * lax.rem(x + 2 - odd, 4) + (y0 + flip) % 2,
+            2 * lax.rem(x + 3 * odd, 4) + (y0 + 1 + flip) % 2,
+        )
+        keys = jnp.concatenate([rop[at(p * 128, 128, 128), :] for p in pairs], axis=0)
+        c = lax.dot_general(lop[...], keys, NT, preferred_element_type=F32).astype(BF)
         for q in range(2):
             for b in range(11):
                 lhs2[q * 64 : q * 64 + 64, b * 128 : b * 128 + 128] = c[b * 64 : b * 64 + 64, q * 128 : q * 128 + 128]
@@ -285,23 +332,24 @@
             zs.append(z.reshape(16, 8, 256))
         for h in range(2):
             z = jnp.concatenate([zs[2 * h], zs[2 * h + 1]], axis=1).astype(BF)
-            sb[h, at(g * 16, 16, 16)] = z
-
-        def scatter_back(s, _):
-            u = (s * 5 + step) % 32
-            t = shifted(me, dx, u % 4, (u // 4 + u) % 4, u // 16)
-            r, cc = t // COLS, t % COLS
-
-            @pl.when(t != me)
-            def _():
-                pltpu.make_async_remote_copy(
-                    src_ref=sb.at[:, cc // 2 * 8 + r, :, at(cc % 2 * 128, 128, 128)], dst_ref=rv.at[me],
-                    send_sem=c_send, recv_sem=c_recv, device_id=dev(t), device_id_type=MESH,
-                ).start()
-
-            return 0
-
-        lax.fori_loop(0, 32, scatter_back, 0)
+            for q in range(2):
+                sb[h, at(pairs[q] * 8, 8, 8)] = z[8 * q : 8 * q + 8]
+
+        for dr in range(ROWS):
+            r = lax.rem(row + dr, ROWS)
+            for k in range(2):
+                for p in pairs:
+
+                    def start(r=r, k=k, p=p):
+                        pltpu.make_async_remote_copy(
+                            src_ref=sb.at[:, p * 8 + r, :, k * 128 : k * 128 + 128], dst_ref=rv.at[me],
+                            send_sem=c_send, recv_sem=c_recv, device_id=(r, 2 * p + k), device_id_type=MESH,
+                        ).start()
+
+                    if dr:
+                        start()
+                    else:
+                        pl.when(2 * p + k != col)(start)
         return 0
 
     lax.fori_loop(0, 4, product, 0)
@@ -324,7 +372,7 @@
             branch = lax.dot_general(n, wout[...], TN, preferred_element_type=F32)
             br[t * 128 : t * 128 + 128] = branch * gate[ia, t * 128 : t * 128 + 128]
         for ib in range(11):
-            cells = pl.ds(11 * ia + ib, CJ, stride=RI)
+            cells = pl.ds(44 * (ia // 4) + in_half(ia % 4, ib), CJ, stride=RI)
             psf[cells, :] = psf[cells, :] + br[44 * ib : 44 * ib + 44]
         return 0
 
@@ -355,7 +403,7 @@
         scratch_shapes=[
             vm((96, 1024), F32), vm((128, 128), F32), vm((16, 768), BF), vm((2, 16, 384), F32), vm((2, 16, 384), BF),
             vm((256, 768), BF), vm((8, 2, 16, 384), BF), vm((256, 384), BF), vm((384, 256), BF), vm((1024, 128), F32),
-            vm((4096, 512), BF), vm((1152, 4096), BF), vm((1152, 512), F32), vm((CJ * RI, 128), F32),
+            vm((4096, 512), BF), vm((1152, 4096), BF), vm((576, 512), F32), vm((CJ * RI, 128), F32),
             vm((8, 512, 128), F32), vm((2, 8 * PITCH, 128), F32), vm((2, 8 * PITCH, 128), F32), vm((512, 128), BF),
             vm((8, 512, 128), F32), vm((N, 4, 16, 128), BF), vm((4, 1024, 256), BF), vm((4, 256, 512), BF),
             vm((4, 512, 256), BF), vm((704, 1024), BF), vm((8, 1024, 128), F32), vm((1024, 1024), BF),
@@ -366,7 +414,7 @@
         compiler_params=pltpu.CompilerParams(
             vmem_limit_bytes=60 * 2**20, collective_id=0, has_side_effects=True
         ),
-    )(hf, ps.transpose(1, 0, 2), f1, f2, wo, wl, wr, wg, wout)
+    )(hf, ps.transpose(1, 0, 2), f1.T, f2.T, wo, wl, wr, wg, wout)
     return out.transpose(1, 0, 2)
 
 

time: 103 us -> 91.9 us (0.89)
  Pallas kernels: 98.3 us -> 89.5 us
  local copies, waits for them, and re-layouts: 4.41 us -> 2.23 us
    pallas_call x1, Pallas kernels: 98.3 us -> 89.5 us  [per_device(): pl.pallas_call(kernel, out_shape=jax.ShapeDtypeStruct((CJ, RI, 128), BF),...]
    unnamed x5 -> x1, local copies, waits for them, and re-layouts: 4.41 us -> 2.23 us
where the time goes in v3:
time: 91.9 us; the launch traced here: 91.7 us
  Pallas kernels  89.5 us (97%)
  local copies, waits for them, and re-layouts  2.23 us (2%)
    pallas_call x1, Pallas kernels, per_device(): pl.pallas_call(kernel, out_shape=jax.ShapeDtypeStruct((CJ, RI, 128), BF),...  89.5 us
    unnamed x1, local copies, waits for them, and re-layouts  2.23 us

profile of v3, /device:TPU:1, one launch (start us, length us, event | category | flops | bytes accessed | tf_op | source)
XLA Modules:
  0.0 91.7 jit_solution(4221976134576511026)
XLA Ops:
  0.0 89.5 %shard_map.91 = bf16[44,88,128]{2,1,0:T(8,128)(2,1)} custom-call(bf16[4,88,256]{2,1,0:T(8,128)(2,1)} %hf.1, bf16[44,88,128]{2,1,0:T(8,128)(2,1)} %bitcast.5, bf16[32,256]{1,0:T(8,128)(2,1)} %bitcast.6, bf16[32,256]{1,0:T(8,128)(2,1)} %bitcast.7, bf16[1024,128]{1,0:T(8,128)(2,1)} %wo.1, bf16[128,256]{1,0:T(8,128)(2,1)} %wl.1, bf16[128,256]{1,0:T(8,128)(2,1)} %wr.1, ...), custom_call_target="tpu_custom_call" | custom-call | tf_op jit(solution)/shard_map/pallas_call | solution.py:398
  89.5 2.2 %copy.11 = bf16[88,44,128]{2,0,1:T(8,128)(2,1)} copy(bf16[88,44,128]{2,0,1:T(8,128)(2,1)} %bitcast.4) | data formatting | bytes 1982464

commit v4 on v3

--- a/solution.py
+++ b/solution.py
@@ -14,6 +14,7 @@
 F32, BF = jnp.float32, jnp.bfloat16
 NT = (((1,), (1,)), ((), ()))
 TN = (((0,), (0,)), ((), ()))
+PARTS = ((0, 6, 0, 2), (6, 11, 2, 4))
 SPAN = ((0, 3), (2, 6), (5, 9), (8, 11))
 
 
@@ -21,10 +22,9 @@
     return 6 * a + b if b < 6 else 24 + 5 * a + b - 6
 
 
-def slot(ia, ib):
-    i = in_half(ia % 4, ib)
-    first = i // 4 if ib < 6 else i // 4 + 6
-    return first + (ia // 4) * (6 if ib < 6 else 5), i % 4
+def slot(a, b, h):
+    i = in_half(a, b) - (0 if b < 6 else 24)
+    return lax.div(i, 4) + h * (6 if b < 6 else 5), lax.rem(i, 4)
 
 
 def group_rows(g):
@@ -53,9 +53,9 @@
 
 def kernel(
     hf, ps, f1, f2, wo, wl, wr, wg, wout, out,
-    a_ref, p_ref, ls, rs32, rs, lmsg, rt, rmsg, rmt, wof, bd, lhs, osc, psf, pn, el, er, wedge, gate,
-    send, lh, sw, s2, lop, rop32, rop, lhs2, sb, rv, rc, br,
-    l_send, l_recv, r1_send, r1_recv, r2_send, r2_recv, e_send, e_recv, c_send, c_recv,
+    a_ref, p_ref, ls, rs32, rs, lmsg, rt, rmsg, rmt, wof, bd, lhs, osc, rsel, psf, pn, el, er, wedge, gate,
+    send, lh, sw, s2, lop, rop32, rop, lhs2, sb, rv, rc, br, psb,
+    p_load, l2_send, l2_recv, l_send, l_recv, r1_send, r1_recv, r2_send, r2_recv, e_send, e_recv, c_send, c_recv,
 ):
     row, col = lax.axis_index("row"), lax.axis_index("col")
     me = row * COLS + col
@@ -66,20 +66,12 @@
     y_row = [lax.div(lax.rem(y + d, 4), 2) * 4 for d in range(4)]
     sem = pltpu.get_barrier_semaphore()
 
-    def greet(o, _):
-        r = lax.rem(row + o, ROWS)
-        for c in range(COLS):
-            if c:
-                pl.semaphore_signal(sem, inc=1, device_id=(r, around[c]), device_id_type=MESH)
-            else:
-
-                @pl.when(o > 0)
-                def _():
-                    pl.semaphore_signal(sem, inc=1, device_id=(r, col), device_id_type=MESH)
-
-        return 0
-
-    lax.fori_loop(0, ROWS, greet, 0)
+    for c in range(1, COLS):
+        pl.semaphore_signal(sem, inc=1, device_id=(row, around[c]), device_id_type=MESH)
+    for r in range(1, ROWS):
+        pl.semaphore_signal(sem, inc=1, device_id=(lax.rem(row + r, ROWS), col), device_id_type=MESH)
+    load = pltpu.make_async_copy(ps, psb, p_load)
+    load.start()
 
     v = hf[...].astype(F32)
     centered = v - jnp.mean(v, axis=-1, keepdims=True)
@@ -113,10 +105,11 @@
                 [tr[s * 32 + eg * 4 : s * 32 + eg * 4 + 4, h * 64 : h * 64 + 48] for eg in range(8)], axis=1
             )
     rs[...] = rs32[...].astype(BF)
-    pl.semaphore_wait(sem, N - 1)
+    pl.semaphore_wait(sem, COLS + ROWS - 2)
 
     own = at(col * 16, 16, 16)
-    pltpu.make_async_copy(ls, lmsg.at[own], l_recv).start()
+    chip, core = lax.div(col, 2), lax.rem(col, 2)
+    pltpu.make_async_copy(ls, lmsg.at[chip, core], l_recv).start()
     pltpu.make_async_copy(rs, rt.at[row], r1_recv).start()
 
     def send_right(s, _):
@@ -130,12 +123,12 @@
 
     def send_left(s, _):
         pltpu.make_async_remote_copy(
-            src_ref=ls, dst_ref=lmsg.at[own], send_sem=l_send, recv_sem=l_recv,
-            device_id=(row, lax.rem(col + s, COLS)), device_id_type=MESH,
+            src_ref=ls, dst_ref=lmsg.at[chip, core], send_sem=l_send, recv_sem=l_recv,
+            device_id=(row, lax.rem(col + 2 * s, COLS)), device_id_type=MESH,
         ).start()
         return 0
 
-    lax.fori_loop(1, COLS, send_left, 0)
+    lax.fori_loop(1, 8, send_left, 0)
 
     wof[...] = wo[...].astype(F32)
     bd[...] = jnp.zeros(bd.shape, BF)
@@ -160,35 +153,34 @@
         return 0
 
     lax.fori_loop(1, COLS, forward_right, 0)
-    psf[...] = ps[...].reshape(CJ * RI, 128).astype(F32)
+    pltpu.make_async_copy(lmsg.at[:, core], lmsg.at[:, core], l_recv).wait()
+    share = pltpu.make_async_remote_copy(
+        src_ref=lmsg.at[:, core], dst_ref=lmsg.at[:, core], send_sem=l2_send, recv_sem=l2_recv,
+        device_id=(row, col + 1 - 2 * core), device_id_type=MESH,
+    )
+    share.start()
+    load.wait()
+    psf[...] = psb[...].reshape(CJ * RI, 128).astype(F32)
     wedge[0:256] = wl[...].T
     wedge[256:512] = wr[...].T
     pltpu.make_async_copy(rmsg, rmsg, r2_recv).wait()
-    pltpu.make_async_copy(lmsg, lmsg, l_recv).wait()
-
     rmt[...] = rmsg[...].T
 
-    def outer(u, _):
+    def pick(u, _):
         a, b = iota((256, 256), 0), iota((256, 256), 1)
         for w in range(4):
-            pick = ones_where((a // 4 == b // 4) & (a % 4 == w) & (b % 4 == u))
-            sel = jnp.dot(rmt[...], pick, preferred_element_type=F32).astype(BF)
-            x = jnp.dot(sel, lmsg[...], preferred_element_type=F32) * (1.0 / 64)
-            for eg in range(8):
-                for qt in range(6):
-                    lhs[
-                        at(qt // 3 * 576 + u * 144 + qt % 3 * 48, 48, 16),
-                        w * 1024 + eg * 128 : w * 1024 + eg * 128 + 128,
-                    ] = x[eg * 48 : eg * 48 + 48, qt * 128 : qt * 128 + 128].astype(BF)
-        return 0
-
-    lax.fori_loop(0, 4, outer, 0)
-
-    def cells_of(half):
-        rows = at(((col // 2) * 8 + row) * 16, 16, 16)
-        return lh.at[2 * half : 2 * half + 2, rows, at(col % 2 * 128, 128, 128)]
-
-    def scatter(half, o):
+            hit = ones_where((a // 4 == b // 4) & (a % 4 == w) & (b % 4 == u))
+            rsel[u, w * 384 : w * 384 + 384] = jnp.dot(rmt[...], hit, preferred_element_type=F32).astype(BF)
+        return 0
+
+    lax.fori_loop(0, 4, pick, 0)
+    share.wait()
+
+
+    def cells_of(m):
+        return lh.at[PARTS[m][2] : PARTS[m][3], at((chip * 8 + row) * 16, 16, 16), at(core * 128, 128, 128)]
+
+    def scatter(m, o):
         z_row = [lax.rem(row + o + d, 4) for d in range(4)]
         k = lax.rem(col + lax.div(o, 4), 2)
         for b in range(4):
@@ -198,8 +190,8 @@
 
                 def start(r=r, c=c):
                     pltpu.make_async_remote_copy(
-                        src_ref=send.at[r * COLS + c, 2 * half : 2 * half + 2], dst_ref=cells_of(half),
-                        send_sem=e_send.at[half], recv_sem=e_recv.at[half], device_id=(r, c), device_id_type=MESH,
+                        src_ref=send.at[r * COLS + c, PARTS[m][2] : PARTS[m][3]], dst_ref=cells_of(m),
+                        send_sem=e_send.at[m], recv_sem=e_recv.at[m], device_id=(r, c), device_id_type=MESH,
                     ).start()
 
                 if a or b:
@@ -207,54 +199,68 @@
                 else:
                     pl.when(o > 0)(start)
 
-    for half in range(2):
-        lo, hi = (0, 6) if half == 0 else (6, 11)
-
-        def project(u, _, half=half):
-            if half:
-                scatter(0, 2 * u)
-                scatter(0, 2 * u + 1)
-            rows = at(half * 576 + u * 288, 288, 16)
-            osc[at(u * 288, 288, 16), :] = jnp.dot(lhs[rows, :], bd[...], preferred_element_type=F32)
+    for m, (lo, hi, t_lo, t_hi) in enumerate(PARTS):
+
+        def outer(u, _, m=m):
+            if m:
+                scatter(m - 1, u)
+            for w in range(4):
+                x = jnp.dot(
+                    rsel[u, w * 384 : w * 384 + 384],
+                    lmsg[:, :, :, m * 384 : m * 384 + 384].reshape(256, 384),
+                    preferred_element_type=F32,
+                ) * (1.0 / 64)
+                for eg in range(8):
+                    for qt in range(3):
+                        lhs[at(u * 144 + qt * 48, 48, 16), w * 1024 + eg * 128 : w * 1024 + eg * 128 + 128] = x[
+                            eg * 48 : eg * 48 + 48, qt * 128 : qt * 128 + 128
+                        ].astype(BF)
             return 0
 
+        lax.fori_loop(0, 4, outer, 0)
+
+        def project(u, _):
+            rows = at(u * 288, 288, 16)
+            osc[rows, :] = jnp.dot(lhs[rows, :], bd[...], preferred_element_type=F32)
+            return 0
+
         lax.fori_loop(0, 2, project, 0)
 
-        def normalize(ia, _, lo=lo, hi=hi, half=half):
-            if half:
-                pl.when(lax.rem(ia, 2) == 0)(lambda: scatter(0, 4 + lax.div(ia, 2)))
+        def normalize(ia, _, m=m, lo=lo, hi=hi, t_lo=t_lo, t_hi=t_hi):
+            if m:
+                pl.when(lax.rem(ia, 2) == 0)(lambda: scatter(m - 1, 4 + lax.div(ia, 2)))
+            h, a = lax.div(ia, 4), lax.rem(ia, 4)
             for ib in range(lo, hi):
-                g, u = slot(ia, ib)
-                g = g - 12 * half
-                upd = osc[at(u * 144 + g // 4 * 48, 48, 8), at(g % 4 * 128, 128, 128)][:44]
-                cells = pl.ds(44 * (ia // 4) + in_half(ia % 4, ib), CJ, stride=RI)
-                m = psf[cells, :] + upd
-                psf[cells, :] = m
-                c = m - jnp.mean(m, axis=-1, keepdims=True)
+                g, u = slot(a, ib, h)
+                upd = osc[at(u * 144 + lax.div(g, 4) * 48, 48, 8), at(lax.rem(g, 4) * 128, 128, 128)][:44]
+                cells = pl.ds(44 * h + in_half(a, ib), CJ, stride=RI)
+                v = psf[cells, :] + upd
+                psf[cells, :] = v
+                c = v - jnp.mean(v, axis=-1, keepdims=True)
                 n = c * lax.rsqrt(jnp.mean(c * c, axis=-1, keepdims=True) + 1e-05)
                 pn[ia, 44 * ib : 44 * ib + 44] = n
-            if half:
+            if hi == 11:
                 pn[ia, 484:512] = jnp.zeros((28, 128), F32)
-            p = pn[ia, half * 256 : half * 256 + 256].astype(BF)
+            p = pn[ia, t_lo * 128 : t_hi * 128].astype(BF)
             proj = lax.dot_general(wedge[...], p, NT, preferred_element_type=F32)
             left = sigmoid(proj[0:128]) * proj[128:256]
             right = sigmoid(proj[256:384]) * proj[384:512]
             rows = at(ia * PITCH, 128, 8)
-            for t in range(2):
+            for t in range(t_hi - t_lo):
                 el[t, rows, :] = left[:, t * 128 : t * 128 + 128]
                 er[t, rows, :] = right[:, t * 128 : t * 128 + 128]
             return 0
 
         lax.fori_loop(0, 8, normalize, 0)
 
-        def pack(c, _, half=half):
-            for t in range(2):
+        def pack(c, _, t_lo=t_lo, t_hi=t_hi):
+            for t in range(t_hi - t_lo):
                 cells = pl.ds(c, 8, stride=PITCH)
-                send[c, 2 * half + t] = jnp.concatenate([el[t, cells, :], er[t, cells, :]], axis=0).astype(BF)
+                send[c, t_lo + t] = jnp.concatenate([el[t, cells, :], er[t, cells, :]], axis=0).astype(BF)
             return 0
 
         lax.fori_loop(0, N, pack, 0, unroll=8)
-        pltpu.make_async_copy(send.at[me, 2 * half : 2 * half + 2], cells_of(half), e_recv.at[half]).start()
+        pltpu.make_async_copy(send.at[me, t_lo:t_hi], cells_of(m), e_recv.at[m]).start()
 
     def scatter_all(o, _):
         scatter(1, o)
@@ -271,7 +277,8 @@
             sw[t, :, (b - lo) * 128 : (b - lo) * 128 + 128] = ones_where(hit)
             n, f = iota((128, 256), 0), iota((128, 256), 1)
             k = n % 16
-            j = jnp.where(k < 6, 6 * (n % 64 // 16) + k, 5 * (n % 64 // 16) + k + 18)
+            a = n % 64 // 16
+            j = jnp.where(k < 6, 6 * a + k, 18 + 5 * a + k)
             hit = (f // 128 == n // 64) & (f % 128 + 128 * t == 44 * b + j) & (k < 11)
             s2[t, (b - lo) * 128 : (b - lo) * 128 + 128, :] = ones_where(hit)
     rop32[...] = jnp.zeros(rop32.shape, F32)
@@ -282,9 +289,9 @@
 
     lax.fori_loop(0, 8, gates, 0)
 
-    for half in range(2):
-        part = lh.at[2 * half : 2 * half + 2]
-        pltpu.make_async_copy(part, part, e_recv.at[half]).wait()
+    for m, (_, _, t_lo, t_hi) in enumerate(PARTS):
+        part = lh.at[t_lo:t_hi]
+        pltpu.make_async_copy(part, part, e_recv.at[m]).wait()
 
     def widen(m, _):
         ys = []
@@ -372,7 +379,7 @@
             branch = lax.dot_general(n, wout[...], TN, preferred_element_type=F32)
             br[t * 128 : t * 128 + 128] = branch * gate[ia, t * 128 : t * 128 + 128]
         for ib in range(11):
-            cells = pl.ds(44 * (ia // 4) + in_half(ia % 4, ib), CJ, stride=RI)
+            cells = pl.ds(44 * lax.div(ia, 4) + in_half(lax.rem(ia, 4), ib), CJ, stride=RI)
             psf[cells, :] = psf[cells, :] + br[44 * ib : 44 * ib + 44]
         return 0
 
@@ -384,11 +391,11 @@
             src_ref=src, dst_ref=src, send_sem=sem, recv_sem=l_recv, device_id=dev((me + 1) % N), device_id_type=MESH
         ).wait_send()
 
-    sent(lmsg.at[0:240], l_send)
+    sent(lmsg.at[0:7, 0], l_send)
     sent(rt.at[0:7], r1_send)
     sent(rmsg.at[0:240], r2_send)
-    for half in range(2):
-        sent(send.at[0 : N - 1, 0:2], e_send.at[half])
+    for m, (_, _, t_lo, t_hi) in enumerate(PARTS):
+        sent(send.at[0 : N - 1, t_lo:t_hi], e_send.at[m])
     sent(rv.at[0 : N - 1], c_send)
 
 
@@ -398,18 +405,18 @@
     out = pl.pallas_call(
         kernel,
         out_shape=jax.ShapeDtypeStruct((CJ, RI, 128), BF),
-        in_specs=[VM] * 9,
+        in_specs=[VM, pl.BlockSpec(memory_space=pl.ANY)] + [VM] * 7,
         out_specs=VM,
         scratch_shapes=[
             vm((96, 1024), F32), vm((128, 128), F32), vm((16, 768), BF), vm((2, 16, 384), F32), vm((2, 16, 384), BF),
-            vm((256, 768), BF), vm((8, 2, 16, 384), BF), vm((256, 384), BF), vm((384, 256), BF), vm((1024, 128), F32),
-            vm((4096, 512), BF), vm((1152, 4096), BF), vm((576, 512), F32), vm((CJ * RI, 128), F32),
+            vm((8, 2, 16, 768), BF), vm((8, 2, 16, 384), BF), vm((256, 384), BF), vm((384, 256), BF), vm((1024, 128), F32),
+            vm((4096, 512), BF), vm((576, 4096), BF), vm((576, 512), F32), vm((4, 1536, 256), BF), vm((CJ * RI, 128), F32),
             vm((8, 512, 128), F32), vm((2, 8 * PITCH, 128), F32), vm((2, 8 * PITCH, 128), F32), vm((512, 128), BF),
             vm((8, 512, 128), F32), vm((N, 4, 16, 128), BF), vm((4, 1024, 256), BF), vm((4, 256, 512), BF),
             vm((4, 512, 256), BF), vm((704, 1024), BF), vm((8, 1024, 128), F32), vm((1024, 1024), BF),
             vm((128, 1408), BF), vm((2, 64, 16, 256), BF), vm((N, 2, 16, 128), BF), vm((2, N * PITCH2, 128), F32),
-            vm((512, 128), F32),
-            dma, dma, dma, dma, dma, dma, dma((2,)), dma((2,)), dma, dma,
+            vm((512, 128), F32), vm((CJ, RI, 128), BF),
+            dma, dma, dma, dma, dma, dma, dma, dma, dma, dma((2,)), dma((2,)), dma, dma,
         ],
         compiler_params=pltpu.CompilerParams(
             vmem_limit_bytes=60 * 2**20, collective_id=0, has_side_effects=True

time: 91.9 us -> 84.8 us (0.923)
  Pallas kernels: 89.5 us -> 82.4 us
    pallas_call x1, Pallas kernels: 89.5 us -> 82.4 us  [per_device(): pl.pallas_call(kernel, out_shape=jax.ShapeDtypeStruct((CJ, RI, 128), BF),...]
where the time goes in v4:
time: 84.8 us; the launch traced here: 84.6 us
  Pallas kernels  82.4 us (97%)
  local copies, waits for them, and re-layouts  2.23 us (3%)
    pallas_call x1, Pallas kernels, per_device(): pl.pallas_call(kernel, out_shape=jax.ShapeDtypeStruct((CJ, RI, 128), BF),...  82.4 us
    unnamed x1, local copies, waits for them, and re-layouts  2.23 us

profile of v4, /device:TPU:1, one launch (start us, length us, event | category | flops | bytes accessed | tf_op | source)
XLA Modules:
  0.0 84.6 jit_solution(6429097147887634271)
XLA Ops:
  0.0 82.4 %shard_map.91 = bf16[44,88,128]{2,1,0:T(8,128)(2,1)} custom-call(bf16[4,88,256]{2,1,0:T(8,128)(2,1)} %hf.1, bf16[44,88,128]{2,1,0:T(8,128)(2,1)} %bitcast.5, bf16[32,256]{1,0:T(8,128)(2,1)} %bitcast.6, bf16[32,256]{1,0:T(8,128)(2,1)} %bitcast.7, bf16[1024,128]{1,0:T(8,128)(2,1)} %wo.1, bf16[128,256]{1,0:T(8,128)(2,1)} %wl.1, bf16[128,256]{1,0:T(8,128)(2,1)} %wr.1, ...), custom_call_target="tpu_custom_call" | custom-call | tf_op jit(solution)/shard_map/pallas_call | solution.py:405
  82.4 2.2 %copy.11 = bf16[88,44,128]{2,0,1:T(8,128)(2,1)} copy(bf16[88,44,128]{2,0,1:T(8,128)(2,1)} %bitcast.4) | data formatting | bytes 1982464

commit v5 on v4

--- a/solution.py
+++ b/solution.py
@@ -251,7 +251,7 @@
                 er[t, rows, :] = right[:, t * 128 : t * 128 + 128]
             return 0
 
-        lax.fori_loop(0, 8, normalize, 0)
+        lax.fori_loop(0, 8, normalize, 0, unroll=2)
 
         def pack(c, _, t_lo=t_lo, t_hi=t_hi):
             for t in range(t_hi - t_lo):
@@ -293,29 +293,26 @@
         part = lh.at[t_lo:t_hi]
         pltpu.make_async_copy(part, part, e_recv.at[m]).wait()
 
-    def widen(m, _):
-        ys = []
-        for t in range(4):
-            lo, hi = SPAN[t]
-            ys.append(
-                jnp.dot(lh[t, at(m * 256, 256, 256), :], sw[t, :, : (hi - lo) * 128], preferred_element_type=F32)
-            )
-        for b in range(11):
-            x = None
-            for t in range(4):
-                lo, hi = SPAN[t]
-                if lo <= b < hi:
-                    y = ys[t][:, (b - lo) * 128 : (b - lo) * 128 + 128]
-                    x = y if x is None else x + y
-            x = x.reshape(2, 8, 2, 8, 128)
-            for q in range(2):
-                p = 2 * m + q
-                lop[b * 64 : b * 64 + 64, at(p * 128, 128, 128)] = x[q, :, 0].reshape(64, 128).astype(BF)
-                for r in range(8):
-                    rop32[p, pl.ds(r * 128 + b, 8, stride=16), :] = x[q, r, 1]
-        return 0
-
-    lax.fori_loop(0, 4, widen, 0)
+        def widen(g, _, m=m):
+            lo, hi = ((0, 5), (5, 11))[m]
+            xs = {}
+            for t in ((0, 1), (1, 2, 3))[m]:
+                first, last = max(SPAN[t][0], lo), min(SPAN[t][1], hi)
+                lanes = slice((first - SPAN[t][0]) * 128, (last - SPAN[t][0]) * 128)
+                y = jnp.dot(lh[t, at(g * 256, 256, 256), :], sw[t, :, lanes], preferred_element_type=F32)
+                for b in range(first, last):
+                    x = y[:, (b - first) * 128 : (b - first) * 128 + 128]
+                    xs[b] = xs[b] + x if b in xs else x
+            for b, x in xs.items():
+                x = x.reshape(2, 8, 2, 8, 128)
+                for q in range(2):
+                    p = 2 * g + q
+                    lop[b * 64 : b * 64 + 64, at(p * 128, 128, 128)] = x[q, :, 0].reshape(64, 128).astype(BF)
+                    for r in range(8):
+                        rop32[p, pl.ds(r * 128 + b, 8, stride=16), :] = x[q, r, 1]
+            return 0
+
+        lax.fori_loop(0, 4, widen, 0)
     for p in range(8):
         rop[:, p * 128 : p * 128 + 128] = rop32[p].astype(BF)
 
@@ -350,7 +347,7 @@
                     def start(r=r, k=k, p=p):
                         pltpu.make_async_remote_copy(
                             src_ref=sb.at[:, p * 8 + r, :, k * 128 : k * 128 + 128], dst_ref=rv.at[me],
-                            send_sem=c_send, recv_sem=c_recv, device_id=(r, 2 * p + k), device_id_type=MESH,
+                            send_sem=c_send, recv_sem=c_recv.at[step], device_id=(r, 2 * p + k), device_id_type=MESH,
                         ).start()
 
                     if dr:
@@ -361,15 +358,23 @@
 
     lax.fori_loop(0, 4, product, 0)
     back = sb.at[:, col // 2 * 8 + row, :, at(col % 2 * 128, 128, 128)]
-    pltpu.make_async_copy(back, rv.at[me], c_recv).start()
-    pltpu.make_async_copy(rv, rv, c_recv).wait()
-
-    def unpack(c, _):
-        for h in range(2):
-            rc[h, at(c * PITCH2, 16, 8), :] = rv[c, h].astype(F32)
-        return 0
-
-    lax.fori_loop(0, N, unpack, 0, unroll=8)
+    pltpu.make_async_copy(back, rv.at[me], c_recv.at[2]).start()
+
+    for step in range(4):
+        odd, flip = step % 2, step // 2
+        part = rv.at[0 : N // 4]
+        pltpu.make_async_copy(part, part, c_recv.at[step]).wait()
+        for dx, dy in ((2 - odd, flip), (3 * odd, 1 + flip)):
+            p = 2 * lax.rem(x + 4 - dx, 4) + lax.rem(y0 + dy, 2)
+
+            def unpack(r, _, p=p):
+                for k in range(2):
+                    c = r * COLS + 2 * p + k
+                    for h in range(2):
+                        rc[h, at(c * PITCH2, 16, 8), :] = rv[c, h].astype(F32)
+                return 0
+
+            lax.fori_loop(0, ROWS, unpack, 0, unroll=4)
 
     def finish(ia, _):
         for t in range(4):
@@ -383,7 +388,7 @@
             psf[cells, :] = psf[cells, :] + br[44 * ib : 44 * ib + 44]
         return 0
 
-    lax.fori_loop(0, 8, finish, 0)
+    lax.fori_loop(0, 8, finish, 0, unroll=2)
     out[...] = psf[...].astype(BF).reshape(CJ, RI, 128)
 
     def sent(src, sem):
@@ -416,7 +421,7 @@
             vm((4, 512, 256), BF), vm((704, 1024), BF), vm((8, 1024, 128), F32), vm((1024, 1024), BF),
             vm((128, 1408), BF), vm((2, 64, 16, 256), BF), vm((N, 2, 16, 128), BF), vm((2, N * PITCH2, 128), F32),
             vm((512, 128), F32), vm((CJ, RI, 128), BF),
-            dma, dma, dma, dma, dma, dma, dma, dma, dma, dma((2,)), dma((2,)), dma, dma,
+            dma, dma, dma, dma, dma, dma, dma, dma, dma, dma((2,)), dma((2,)), dma, dma((4,)),
         ],
         compiler_params=pltpu.CompilerParams(
             vmem_limit_bytes=60 * 2**20, collective_id=0, has_side_effects=True

time: 84.8 us -> 81.9 us (0.966)
  Pallas kernels: 82.4 us -> 79.5 us
    pallas_call x1, Pallas kernels: 82.4 us -> 79.5 us  [per_device(): pl.pallas_call(kernel, out_shape=jax.ShapeDtypeStruct((CJ, RI, 128), BF),...]
where the time goes in v5:
time: 81.9 us; the launch traced here: 81.8 us
  Pallas kernels  79.5 us (97%)
  local copies, waits for them, and re-layouts  2.23 us (3%)
    pallas_call x1, Pallas kernels, per_device(): pl.pallas_call(kernel, out_shape=jax.ShapeDtypeStruct((CJ, RI, 128), BF),...  79.5 us
    unnamed x1, local copies, waits for them, and re-layouts  2.23 us

profile of v5, /device:TPU:1, one launch (start us, length us, event | category | flops | bytes accessed | tf_op | source)
XLA Modules:
  0.0 81.8 jit_solution(12675629006407499867)
XLA Ops:
  0.0 79.5 %shard_map.91 = bf16[44,88,128]{2,1,0:T(8,128)(2,1)} custom-call(bf16[4,88,256]{2,1,0:T(8,128)(2,1)} %hf.1, bf16[44,88,128]{2,1,0:T(8,128)(2,1)} %bitcast.5, bf16[32,256]{1,0:T(8,128)(2,1)} %bitcast.6, bf16[32,256]{1,0:T(8,128)(2,1)} %bitcast.7, bf16[1024,128]{1,0:T(8,128)(2,1)} %wo.1, bf16[128,256]{1,0:T(8,128)(2,1)} %wl.1, bf16[128,256]{1,0:T(8,128)(2,1)} %wr.1, ...), custom_call_target="tpu_custom_call" | custom-call | tf_op jit(solution)/shard_map/pallas_call | solution.py:410
  79.5 2.2 %copy.11 = bf16[88,44,128]{2,0,1:T(8,128)(2,1)} copy(bf16[88,44,128]{2,0,1:T(8,128)(2,1)} %bitcast.4) | data formatting | bytes 1982464

commit v6 on v5

--- a/solution.py
+++ b/solution.py
@@ -52,10 +52,11 @@
 
 
 def kernel(
-    hf, ps, f1, f2, wo, wl, wr, wg, wout, out,
+    hf_any, ps_any, f1_any, f2_any, wo_any, wl_any, wr_any, wg_any, wout_any, out,
+    hf, ps, f1, f2, wo, wl, wr, wg, wout,
     a_ref, p_ref, ls, rs32, rs, lmsg, rt, rmsg, rmt, wof, bd, lhs, osc, rsel, psf, pn, el, er, wedge, gate,
-    send, lh, sw, s2, lop, rop32, rop, lhs2, sb, rv, rc, br, psb,
-    p_load, l2_send, l2_recv, l_send, l_recv, r1_send, r1_recv, r2_send, r2_recv, e_send, e_recv, c_send, c_recv,
+    send, lh, sw, s2, lop, rop32, rop, lhs2, sb, rv, rc, br,
+    loaded, l2_send, l2_recv, l_send, l_recv, r1_send, r1_recv, r2_send, r2_recv, e_send, e_recv, c_send, c_recv,
 ):
     row, col = lax.axis_index("row"), lax.axis_index("col")
     me = row * COLS + col
@@ -66,16 +67,56 @@
     y_row = [lax.div(lax.rem(y + d, 4), 2) * 4 for d in range(4)]
     sem = pltpu.get_barrier_semaphore()
 
+    loads = [
+        pltpu.make_async_copy(src, dst, loaded.at[n])
+        for n, (src, dst) in enumerate(
+            (
+                (hf_any, hf), (f2_any, f2), (f1_any, f1), (wo_any, wo), (ps_any, ps), (wl_any, wl), (wr_any, wr),
+                (wg_any, wg), (wout_any, wout),
+            )
+        )
+    ]
+    for load in loads:
+        load.start()
+
     for c in range(1, COLS):
         pl.semaphore_signal(sem, inc=1, device_id=(row, around[c]), device_id_type=MESH)
     for r in range(1, ROWS):
         pl.semaphore_signal(sem, inc=1, device_id=(lax.rem(row + r, ROWS), col), device_id_type=MESH)
-    load = pltpu.make_async_copy(ps, psb, p_load)
-    load.start()
-
+
+    for load in loads[:3]:
+        load.wait()
     v = hf[...].astype(F32)
     centered = v - jnp.mean(v, axis=-1, keepdims=True)
     mn = centered * lax.rsqrt(jnp.mean(centered * centered, axis=-1, keepdims=True) + 1e-05)
+    pr = jnp.concatenate(
+        [lax.dot_general(mn[s].astype(BF), f2[...], NT, preferred_element_type=F32) for s in range(4)], axis=1
+    )
+    p_ref[...] = jnp.zeros(p_ref.shape, F32)
+    p_ref[0:44] = pr[0:44]
+    p_ref[64:108] = pr[44:88]
+    tr = p_ref[...].T
+    for h in range(2):
+        for s in range(4):
+            rs32[h, s * 4 : s * 4 + 4, :] = jnp.concatenate(
+                [tr[s * 32 + eg * 4 : s * 32 + eg * 4 + 4, h * 64 : h * 64 + 48] for eg in range(8)], axis=1
+            )
+    rs[...] = rs32[...].astype(BF)
+    pl.semaphore_wait(sem, COLS + ROWS - 2)
+
+    own = at(col * 16, 16, 16)
+    chip, core = lax.div(col, 2), lax.rem(col, 2)
+    pltpu.make_async_copy(rs, rt.at[row], r1_recv).start()
+
+    def send_right(s, _):
+        pltpu.make_async_remote_copy(
+            src_ref=rs, dst_ref=rt.at[row], send_sem=r1_send, recv_sem=r1_recv,
+            device_id=(lax.rem(row + s, ROWS), col), device_id_type=MESH,
+        ).start()
+        return 0
+
+    lax.fori_loop(1, ROWS, send_right, 0)
+
     for s in range(4):
         for g in range(22):
             qt, q = g // 4, g % 4
@@ -92,34 +133,7 @@
     )
     for qt in range(6):
         ls[:, qt * 128 : qt * 128 + 128] = lm[qt * 16 : qt * 16 + 16].astype(BF)
-    pr = jnp.concatenate(
-        [lax.dot_general(mn[s].astype(BF), f2[...], NT, preferred_element_type=F32) for s in range(4)], axis=1
-    )
-    p_ref[...] = jnp.zeros(p_ref.shape, F32)
-    p_ref[0:44] = pr[0:44]
-    p_ref[64:108] = pr[44:88]
-    tr = p_ref[...].T
-    for h in range(2):
-        for s in range(4):
-            rs32[h, s * 4 : s * 4 + 4, :] = jnp.concatenate(
-                [tr[s * 32 + eg * 4 : s * 32 + eg * 4 + 4, h * 64 : h * 64 + 48] for eg in range(8)], axis=1
-            )
-    rs[...] = rs32[...].astype(BF)
-    pl.semaphore_wait(sem, COLS + ROWS - 2)
-
-    own = at(col * 16, 16, 16)
-    chip, core = lax.div(col, 2), lax.rem(col, 2)
     pltpu.make_async_copy(ls, lmsg.at[chip, core], l_recv).start()
-    pltpu.make_async_copy(rs, rt.at[row], r1_recv).start()
-
-    def send_right(s, _):
-        pltpu.make_async_remote_copy(
-            src_ref=rs, dst_ref=rt.at[row], send_sem=r1_send, recv_sem=r1_recv,
-            device_id=(lax.rem(row + s, ROWS), col), device_id_type=MESH,
-        ).start()
-        return 0
-
-    lax.fori_loop(1, ROWS, send_right, 0)
 
     def send_left(s, _):
         pltpu.make_async_remote_copy(
@@ -130,16 +144,6 @@
 
     lax.fori_loop(1, 8, send_left, 0)
 
-    wof[...] = wo[...].astype(F32)
-    bd[...] = jnp.zeros(bd.shape, BF)
-
-    def place(b, _):
-        w = wof[pl.ds((b % 8) * 4 + b // 8, 32, stride=32), :].astype(BF)
-        for q in range(4):
-            bd[at(b * 128 + q * 32, 32, 32), q * 128 : q * 128 + 128] = w
-        return 0
-
-    lax.fori_loop(0, 32, place, 0, unroll=4)
     pltpu.make_async_copy(rt, rt, r1_recv).wait()
     own_half = pltpu.make_async_copy(rt.at[col // 2, col % 2], rmsg.at[own], r2_recv)
     own_half.start()
@@ -159,8 +163,19 @@
         device_id=(row, col + 1 - 2 * core), device_id_type=MESH,
     )
     share.start()
-    load.wait()
-    psf[...] = psb[...].reshape(CJ * RI, 128).astype(F32)
+    for load in loads[3:]:
+        load.wait()
+    wof[...] = wo[...].astype(F32)
+    bd[...] = jnp.zeros(bd.shape, BF)
+
+    def place(b, _):
+        w = wof[pl.ds((b % 8) * 4 + b // 8, 32, stride=32), :].astype(BF)
+        for q in range(4):
+            bd[at(b * 128 + q * 32, 32, 32), q * 128 : q * 128 + 128] = w
+        return 0
+
+    lax.fori_loop(0, 32, place, 0, unroll=4)
+    psf[...] = ps[...].reshape(CJ * RI, 128).astype(F32)
     wedge[0:256] = wl[...].T
     wedge[256:512] = wr[...].T
     pltpu.make_async_copy(rmsg, rmsg, r2_recv).wait()
@@ -173,7 +188,7 @@
             rsel[u, w * 384 : w * 384 + 384] = jnp.dot(rmt[...], hit, preferred_element_type=F32).astype(BF)
         return 0
 
-    lax.fori_loop(0, 4, pick, 0)
+    lax.fori_loop(0, 4, pick, 0, unroll=4)
     share.wait()
 
 
@@ -217,7 +232,7 @@
                         ].astype(BF)
             return 0
 
-        lax.fori_loop(0, 4, outer, 0)
+        lax.fori_loop(0, 4, outer, 0, unroll=2)
 
         def project(u, _):
             rows = at(u * 288, 288, 16)
@@ -251,7 +266,7 @@
                 er[t, rows, :] = right[:, t * 128 : t * 128 + 128]
             return 0
 
-        lax.fori_loop(0, 8, normalize, 0, unroll=2)
+        lax.fori_loop(0, 8, normalize, 0, unroll=4)
 
         def pack(c, _, t_lo=t_lo, t_hi=t_hi):
             for t in range(t_hi - t_lo):
@@ -312,7 +327,7 @@
                         rop32[p, pl.ds(r * 128 + b, 8, stride=16), :] = x[q, r, 1]
             return 0
 
-        lax.fori_loop(0, 4, widen, 0)
+        lax.fori_loop(0, 4, widen, 0, unroll=2)
     for p in range(8):
         rop[:, p * 128 : p * 128 + 128] = rop32[p].astype(BF)
 
@@ -388,7 +403,7 @@
             psf[cells, :] = psf[cells, :] + br[44 * ib : 44 * ib + 44]
         return 0
 
-    lax.fori_loop(0, 8, finish, 0, unroll=2)
+    lax.fori_loop(0, 8, finish, 0, unroll=4)
     out[...] = psf[...].astype(BF).reshape(CJ, RI, 128)
 
     def sent(src, sem):
@@ -410,9 +425,11 @@
     out = pl.pallas_call(
         kernel,
         out_shape=jax.ShapeDtypeStruct((CJ, RI, 128), BF),
-        in_specs=[VM, pl.BlockSpec(memory_space=pl.ANY)] + [VM] * 7,
+        in_specs=[pl.BlockSpec(memory_space=pl.ANY)] * 9,
         out_specs=VM,
         scratch_shapes=[
+            vm(hf.shape, BF), vm((CJ, RI, 128), BF), vm((32, 256), BF), vm((32, 256), BF), vm(wo.shape, BF),
+            vm(wl.shape, BF), vm(wr.shape, BF), vm(wg.shape, BF), vm(wout.shape, BF),
             vm((96, 1024), F32), vm((128, 128), F32), vm((16, 768), BF), vm((2, 16, 384), F32), vm((2, 16, 384), BF),
             vm((8, 2, 16, 768), BF), vm((8, 2, 16, 384), BF), vm((256, 384), BF), vm((384, 256), BF), vm((1024, 128), F32),
             vm((4096, 512), BF), vm((576, 4096), BF), vm((576, 512), F32), vm((4, 1536, 256), BF), vm((CJ * RI, 128), F32),
@@ -420,8 +437,7 @@
             vm((8, 512, 128), F32), vm((N, 4, 16, 128), BF), vm((4, 1024, 256), BF), vm((4, 256, 512), BF),
             vm((4, 512, 256), BF), vm((704, 1024), BF), vm((8, 1024, 128), F32), vm((1024, 1024), BF),
             vm((128, 1408), BF), vm((2, 64, 16, 256), BF), vm((N, 2, 16, 128), BF), vm((2, N * PITCH2, 128), F32),
-            vm((512, 128), F32), vm((CJ, RI, 128), BF),
-            dma, dma, dma, dma, dma, dma, dma, dma, dma, dma((2,)), dma((2,)), dma, dma((4,)),
+            vm((512, 128), F32), dma((9,)), dma, dma, dma, dma, dma, dma, dma, dma, dma((2,)), dma((2,)), dma, dma((4,)),
         ],
         compiler_params=pltpu.CompilerParams(
             vmem_limit_bytes=60 * 2**20, collective_id=0, has_side_effects=True

time: 81.9 us -> 78.6 us (0.960)
  Pallas kernels: 79.5 us -> 76.3 us
    pallas_call x1, Pallas kernels: 79.5 us -> 76.3 us  [per_device(): pl.pallas_call(kernel, out_shape=jax.ShapeDtypeStruct((CJ, RI, 128), BF),...]
where the time goes in v6:
time: 78.6 us; the launch traced here: 78.5 us
  Pallas kernels  76.3 us (97%)
  local copies, waits for them, and re-layouts  2.23 us (3%)
    pallas_call x1, Pallas kernels, per_device(): pl.pallas_call(kernel, out_shape=jax.ShapeDtypeStruct((CJ, RI, 128), BF),...  76.3 us
    unnamed x1, local copies, waits for them, and re-layouts  2.23 us

profile of v6, /device:TPU:1, one launch (start us, length us, event | category | flops | bytes accessed | tf_op | source)
XLA Modules:
  0.0 78.5 jit_solution(5261312828882701594)
XLA Ops:
  0.0 76.3 %shard_map.91 = bf16[44,88,128]{2,1,0:T(8,128)(2,1)} custom-call(bf16[4,88,256]{2,1,0:T(8,128)(2,1)} %hf_any.1, bf16[44,88,128]{2,1,0:T(8,128)(2,1)} %bitcast.5, bf16[32,256]{1,0:T(8,128)(2,1)} %bitcast.6, bf16[32,256]{1,0:T(8,128)(2,1)} %bitcast.7, bf16[1024,128]{1,0:T(8,128)(2,1)} %wo_any.1, bf16[128,256]{1,0:T(8,128)(2,1)} %wl_any.1, ...), custom_call_target="tpu_custom_call" | custom-call | tf_op jit(solution)/shard_map/pallas_call | solution.py:425
  76.3 2.2 %copy.11 = bf16[88,44,128]{2,0,1:T(8,128)(2,1)} copy(bf16[88,44,128]{2,0,1:T(8,128)(2,1)} %bitcast.4) | data formatting | bytes 1982464

commit v7 on v6

--- a/solution.py
+++ b/solution.py
@@ -232,14 +232,14 @@
                         ].astype(BF)
             return 0
 
-        lax.fori_loop(0, 4, outer, 0, unroll=2)
+        lax.fori_loop(0, 4, outer, 0, unroll=4)
 
         def project(u, _):
             rows = at(u * 288, 288, 16)
             osc[rows, :] = jnp.dot(lhs[rows, :], bd[...], preferred_element_type=F32)
             return 0
 
-        lax.fori_loop(0, 2, project, 0)
+        lax.fori_loop(0, 2, project, 0, unroll=2)
 
         def normalize(ia, _, m=m, lo=lo, hi=hi, t_lo=t_lo, t_hi=t_hi):
             if m:
@@ -266,7 +266,7 @@
                 er[t, rows, :] = right[:, t * 128 : t * 128 + 128]
             return 0
 
-        lax.fori_loop(0, 8, normalize, 0, unroll=4)
+        lax.fori_loop(0, 8, normalize, 0, unroll=8)
 
         def pack(c, _, t_lo=t_lo, t_hi=t_hi):
             for t in range(t_hi - t_lo):
@@ -274,7 +274,7 @@
                 send[c, t_lo + t] = jnp.concatenate([el[t, cells, :], er[t, cells, :]], axis=0).astype(BF)
             return 0
 
-        lax.fori_loop(0, N, pack, 0, unroll=8)
+        lax.fori_loop(0, N, pack, 0, unroll=16)
         pltpu.make_async_copy(send.at[me, t_lo:t_hi], cells_of(m), e_recv.at[m]).start()
 
     def scatter_all(o, _):
@@ -403,7 +403,7 @@
             psf[cells, :] = psf[cells, :] + br[44 * ib : 44 * ib + 44]
         return 0
 
-    lax.fori_loop(0, 8, finish, 0, unroll=4)
+    lax.fori_loop(0, 8, finish, 0, unroll=8)
     out[...] = psf[...].astype(BF).reshape(CJ, RI, 128)
 
     def sent(src, sem):

time: 78.6 us -> 77.1 us (0.981)
  Pallas kernels: 76.3 us -> 74.7 us
    pallas_call x1, Pallas kernels: 76.3 us -> 74.7 us  [per_device(): pl.pallas_call(kernel, out_shape=jax.ShapeDtypeStruct((CJ, RI, 128), BF),...]
where the time goes in v7:
time: 77.1 us; the launch traced here: 76.9 us
  Pallas kernels  74.7 us (97%)
  local copies, waits for them, and re-layouts  2.23 us (3%)
    pallas_call x1, Pallas kernels, per_device(): pl.pallas_call(kernel, out_shape=jax.ShapeDtypeStruct((CJ, RI, 128), BF),...  74.7 us
    unnamed x1, local copies, waits for them, and re-layouts  2.23 us

profile of v7, /device:TPU:1, one launch (start us, length us, event | category | flops | bytes accessed | tf_op | source)
XLA Modules:
  0.0 76.9 jit_solution(10954847984448920417)
XLA Ops:
  0.0 74.7 %shard_map.91 = bf16[44,88,128]{2,1,0:T(8,128)(2,1)} custom-call(bf16[4,88,256]{2,1,0:T(8,128)(2,1)} %hf_any.1, bf16[44,88,128]{2,1,0:T(8,128)(2,1)} %bitcast.5, bf16[32,256]{1,0:T(8,128)(2,1)} %bitcast.6, bf16[32,256]{1,0:T(8,128)(2,1)} %bitcast.7, bf16[1024,128]{1,0:T(8,128)(2,1)} %wo_any.1, bf16[128,256]{1,0:T(8,128)(2,1)} %wl_any.1, ...), custom_call_target="tpu_custom_call" | custom-call | tf_op jit(solution)/shard_map/pallas_call | solution.py:425
  74.7 2.2 %copy.11 = bf16[88,44,128]{2,0,1:T(8,128)(2,1)} copy(bf16[88,44,128]{2,0,1:T(8,128)(2,1)} %bitcast.4) | data formatting | bytes 1982464

commit v8 on v7

--- a/solution.py
+++ b/solution.py
@@ -174,7 +174,7 @@
             bd[at(b * 128 + q * 32, 32, 32), q * 128 : q * 128 + 128] = w
         return 0
 
-    lax.fori_loop(0, 32, place, 0, unroll=4)
+    lax.fori_loop(0, 32, place, 0, unroll=16)
     psf[...] = ps[...].reshape(CJ * RI, 128).astype(F32)
     wedge[0:256] = wl[...].T
     wedge[256:512] = wr[...].T
@@ -327,7 +327,7 @@
                         rop32[p, pl.ds(r * 128 + b, 8, stride=16), :] = x[q, r, 1]
             return 0
 
-        lax.fori_loop(0, 4, widen, 0, unroll=2)
+        lax.fori_loop(0, 4, widen, 0, unroll=4)
     for p in range(8):
         rop[:, p * 128 : p * 128 + 128] = rop32[p].astype(BF)
 
@@ -371,7 +371,7 @@
                         pl.when(2 * p + k != col)(start)
         return 0
 
-    lax.fori_loop(0, 4, product, 0)
+    lax.fori_loop(0, 4, product, 0, unroll=2)
     back = sb.at[:, col // 2 * 8 + row, :, at(col % 2 * 128, 128, 128)]
     pltpu.make_async_copy(back, rv.at[me], c_recv.at[2]).start()
 

time: 77.1 us -> 76.9 us (level)
  no operation moved by 1% of the time
where the time goes in v8:
time: 76.9 us; the launch traced here: 76.8 us
  Pallas kernels  74.5 us (97%)
  local copies, waits for them, and re-layouts  2.23 us (3%)
    pallas_call x1, Pallas kernels, per_device(): pl.pallas_call(kernel, out_shape=jax.ShapeDtypeStruct((CJ, RI, 128), BF),...  74.5 us
    unnamed x1, local copies, waits for them, and re-layouts  2.23 us

profile of v8, /device:TPU:1, one launch (start us, length us, event | category | flops | bytes accessed | tf_op | source)
XLA Modules:
  0.0 76.8 jit_solution(18268970227171755341)
XLA Ops:
  0.0 74.5 %shard_map.91 = bf16[44,88,128]{2,1,0:T(8,128)(2,1)} custom-call(bf16[4,88,256]{2,1,0:T(8,128)(2,1)} %hf_any.1, bf16[44,88,128]{2,1,0:T(8,128)(2,1)} %bitcast.5, bf16[32,256]{1,0:T(8,128)(2,1)} %bitcast.6, bf16[32,256]{1,0:T(8,128)(2,1)} %bitcast.7, bf16[1024,128]{1,0:T(8,128)(2,1)} %wo_any.1, bf16[128,256]{1,0:T(8,128)(2,1)} %wl_any.1, ...), custom_call_target="tpu_custom_call" | custom-call | tf_op jit(solution)/shard_map/pallas_call | solution.py:425
  74.5 2.2 %copy.11 = bf16[88,44,128]{2,0,1:T(8,128)(2,1)} copy(bf16[88,44,128]{2,0,1:T(8,128)(2,1)} %bitcast.4) | data formatting | bytes 1982464
